TPU v7x, 256 devices: a whole 4x4x8 slice. The times are simulated.
256 devices in a mesh: sec: 2 (over z_hi), seq: 16 (over y, z_lo), tp: 8 (over x, core).
Axes of the slice: x: 4, y: 4, z: 8 (z_hi: 2, z_lo: 4; z = z_hi * 4 + z_lo), core: 2. Of those that a mesh axis runs over, the one named last changes fastest.
Arguments:
- hidden_context: bfloat16 [8192, 8192], P(('sec', 'seq'), 'tp')
- hidden_rows: bfloat16 [512, 8192], P(('sec', 'seq'), 'tp')
- norm_gain: float32 [8192], replicated, may hold values from 0.25 to 2
- key_value_weight: bfloat16 [8192, 2, 1024], P(None, None, 'tp'), may hold values from -0.0625 to 0.0625
- value_bias: float32 [1024], P('tp'), may hold values from -4 to 4
- query_context: bfloat16 [8192, 8192], P(('sec', 'seq'), 'tp')
- query_rows: bfloat16 [512, 8192], P(('sec', 'seq'), 'tp')
- context_length: int32 [512], P(('sec', 'seq')), may hold values from 1 to 8192, as said below
- row_node: int32 [512], replicated, may hold values from 0 to 255, never falling along the last dimension, each value on 1 to 4 neighbouring positions
Outputs:
- prefill_attended: bfloat16 [8192, 8192], P(('sec', 'seq'), 'tp')
- decode_attended: bfloat16 [512, 8192], P(('sec', 'seq'), 'tp')
Inputs may be any that keep to these rules, and one draw needn't show every extreme that they name: `context_length`: some row sees the whole context of 8192 tokens. `row_node`: never falls; each node holds 1 to 4 consecutive rows, and some node exactly 4.
All inputs are finite; a program needn't handle non-finite values.
Results may differ from a plain program's by a relative error of at most 0.012.
The roundings to bfloat16 on the way count: a program that leaves them out, or rounds other values in their place, can miss the bound.
Values may be sent and summed in bfloat16 or wider, within the bound.
No kernel may reach another device: no remote copies, remote signals or barrier semaphores. Data moves between devices by JAX's collectives and lax.ppermute only.
A program may use at most 64 MiB of HBM per device.

v0:
```python
import functools
import math

import jax
import jax.numpy as jnp
from jax import lax
from jax.experimental import pallas as pl
from jax.experimental.pallas import tpu as pltpu
from jax.sharding import PartitionSpec as P

D = 8192
H = 64
KVH = 8
HD = 128
STEPS = 4
GROUP = H // KVH

PLACE = ("sec", "seq")
RING_Z, RING_Y, RUN = 8, 4, 4
TOK = 256
ROW = 16
BOTH = TOK + ROW
TOP = 128
WIDE = 1024
HEIGHT = GROUP * (TOK + ROW)
LEVELS = 32
LOWEST = -1e30
SCALE = math.log2(math.e) / math.sqrt(HD)
VMEM = 32 * 1024 * 1024
IN_VMEM = pl.BlockSpec(memory_space=pltpu.VMEM)
IN_SMEM = pl.BlockSpec(memory_space=pltpu.SMEM)
IN_HBM = pl.BlockSpec(memory_space=pltpu.HBM)


def place_of(y, z):
    return (z // RUN) * (RING_Y * RUN) + y * RUN + z % RUN


def move(block, dz, dy):
    route = [
        (place_of(y, z), place_of((y + dy) % RING_Y, (z + dz) % RING_Z))
        for y in range(RING_Y)
        for z in range(RING_Z)
    ]
    return lax.ppermute(block, PLACE, route)


def move_x(block, step):
    return lax.ppermute(block, "tp", [(i, (i + 2 * step) % 8) for i in range(8)])


def swap_core(block):
    return lax.ppermute(block, "tp", [(i, i ^ 1) for i in range(8)])


def project_kernel(spans, shifts, later, held, first, last, tp_ref, *refs):
    refs = list(refs)
    pieces = [[(refs.pop(0), *span) for span in piece] for piece in spans]
    weights, gain = refs.pop(0), refs.pop(0)
    if not first:
        product_in, squares_in = refs.pop(0), refs.pop(0)
    if last:
        bias = refs.pop(0)
    tp = tp_ref[0]
    mate = tp + 1 - 2 * (tp % 2)

    def owner_of(shift):
        step, other = shift
        return ((mate if other else tp) + 2 * step + 8) % 8

    copies = []
    if held is None:
        ready, slices = refs.pop(), refs.pop()
        for number, shift in enumerate(shifts + later):
            rows = pl.ds(pl.multiple_of(owner_of(shift) * WIDE, WIDE), WIDE)
            far = number - len(shifts)
            to = slices.at[number] if far < 0 else refs[2].at[far]
            copies.append(pltpu.make_async_copy(weights.at[rows, :], to, ready.at[number]))
            copies[-1].start()
    else:
        slices = weights
    product = jnp.zeros((BOTH, 2 * HD), jnp.float32) if first else product_in[...]
    squares = jnp.zeros((BOTH, HD), jnp.float32) if first else squares_in[...]
    for number, (piece, shift) in enumerate(zip(pieces, shifts)):
        if held is None:
            copies[number].wait()
        slot = number if held is None else held[number]

        def chunk(turn, carry, piece=piece, slot=slot, owner=owner_of(shift)):
            product, squares = carry
            span = pl.ds(pl.multiple_of(turn * 256, 256), 256)
            chunks = [ref[pl.ds(start, stop - start), span] for ref, start, stop in piece]
            wide = jnp.concatenate(chunks, axis=0).astype(jnp.float32)
            squared = wide * wide
            squares = squares + (squared[:, :HD] + squared[:, HD:])
            scaled = (wide * gain[pl.ds(owner, 1), span]).astype(jnp.bfloat16)
            return (
                product
                + jnp.dot(scaled, slices[slot, span, :], preferred_element_type=jnp.float32),
                squares,
            )

        if len(pieces) == 1:
            for number in range(WIDE // 256):
                product, squares = chunk(number, (product, squares))
        else:
            product, squares = lax.fori_loop(0, WIDE // 256, chunk, (product, squares))
    for copy in copies[len(shifts) :]:
        copy.wait()
    if not last:
        refs[0][...] = product
        refs[1][...] = squares
        return
    inverse = lax.rsqrt(jnp.sum(squares, axis=1, keepdims=True) / D + 1e-06)
    keys = (product[:, :HD] * inverse).astype(jnp.bfloat16)
    values = (product[:, HD:] * inverse + bias[...]).astype(jnp.bfloat16)
    refs[0][:, :HD] = keys[:TOK]
    refs[0][:, HD:] = values[:TOK]
    refs[1][:, :HD] = keys[TOK:]
    refs[1][:, HD:] = values[TOK:]


def project(tp, gain, pieces, shifts, weights, later=(), held=None, state=None, bias=None):
    spans = [[(start, stop) for _, start, stop in piece] for piece in pieces]
    count, later = len(pieces), list(later)
    first, last = state is None, bias is not None
    operands = [tp] + [chunk[0] for piece in pieces for chunk in piece] + [weights, gain]
    specs = [IN_SMEM] + [IN_VMEM] * (len(operands) - 3)
    specs += [IN_HBM if held is None else IN_VMEM, IN_VMEM]
    if not first:
        operands += list(state)
    if last:
        operands.append(bias)
        shapes = [
            jax.ShapeDtypeStruct((TOK, 2 * HD), jnp.bfloat16),
            jax.ShapeDtypeStruct((ROW, 2 * HD), jnp.bfloat16),
        ]
    else:
        shapes = [
            jax.ShapeDtypeStruct((BOTH, 2 * HD), jnp.float32),
            jax.ShapeDtypeStruct((BOTH, HD), jnp.float32),
        ]
    if later:
        shapes.append(jax.ShapeDtypeStruct((len(later), WIDE, 2 * HD), jnp.bfloat16))
    scratch = []
    if held is None:
        scratch = [
            pltpu.VMEM((count, WIDE, 2 * HD), jnp.bfloat16),
            pltpu.SemaphoreType.DMA((count + len(later),)),
        ]
    specs += [IN_VMEM] * (len(operands) - len(specs))
    results = pl.pallas_call(
        functools.partial(project_kernel, spans, shifts, later, held, first, last),
        in_specs=specs,
        out_specs=[IN_VMEM] * len(shapes),
        out_shape=shapes,
        scratch_shapes=scratch,
        compiler_params=pltpu.CompilerParams(vmem_limit_bytes=VMEM),
        cost_estimate=pl.CostEstimate(
            flops=count * BOTH * WIDE * 512,
            bytes_accessed=count * 1100000,
            transcendentals=0,
        ),
    )(*operands)
    return (tuple(results[:2]), results[2]) if later else tuple(results)


def attend(queries, keys, values, allowed, guard, top_ref, mixed_ref, rows, active=None):
    parts = []
    highest = None
    for number in range(len(keys)):
        scores = lax.dot_general(
            queries, keys[number], (((1,), (1,)), ((), ())), preferred_element_type=jnp.float32
        )
        scores = scores * SCALE
        if allowed is not None:
            scores = jnp.where(allowed[number], scores, LOWEST)
        parts.append(scores)
        for begin in range(0, scores.shape[1], HD):
            piece = scores[:, begin : begin + HD]
            highest = piece if highest is None else jnp.maximum(highest, piece)
    before = top_ref[rows, :]
    top = jnp.maximum(before, jnp.max(highest, axis=1, keepdims=True))
    factor = jnp.exp2(before - top)
    earlier = mixed_ref[rows, :]
    mixed = earlier * jnp.concatenate([factor, factor], axis=1)
    for number in range(len(keys)):
        width = parts[number].shape[1]
        lifted = jnp.concatenate([top] * (width // HD), axis=1)
        weight = jnp.exp2(parts[number] - lifted)
        if guard:
            weight = jnp.where(allowed[number], weight, 0.0)
        mixed = mixed + jnp.dot(
            weight.astype(jnp.bfloat16), values[number], preferred_element_type=jnp.float32
        )
    if active is not None:
        top, mixed = jnp.where(active, top, before), jnp.where(active, mixed, earlier)
    top_ref[rows, :] = top
    mixed_ref[rows, :] = mixed


def per_row(table, begin):
    seat = lax.broadcasted_iota(jnp.int32, (ROW, HD), 0)
    found = jnp.zeros((ROW, HD), jnp.int32)
    for row in range(ROW):
        found = jnp.where(seat == row, table[begin + row], found)
    return found


def head_rows(pack):
    rows = pack[TOK : TOK + ROW, :]
    return [rows[:, head * HD : (head + 1) * HD] for head in range(GROUP)]


def reach_of(pack):
    coded = pack[TOK + ROW :, : 2 * HD].astype(jnp.float32)
    return coded[:, :HD] * 64.0 + coded[:, HD:]


def diagonal():
    row = lax.broadcasted_iota(jnp.int32, (HD, HD), 0)
    return row == lax.broadcasted_iota(jnp.int32, (HD, HD), 1)


def seal(top_ref, mixed_ref, begin, count, to, packed, levels):
    rows = slice(begin, begin + count)
    mixed = mixed_ref[rows, :]
    amount = mixed[:, HD:]
    some = amount > 0.0
    safe = jnp.where(some, amount, 1.0)
    packed[to : to + count, :] = (mixed[:, :HD] / safe).astype(jnp.bfloat16)
    level = jnp.where(some, top_ref[rows, :] + jnp.log2(safe), LOWEST)
    seat = lax.broadcasted_iota(jnp.int32, levels.shape, 0)
    for start in range(0, count, HD):
        flat = jnp.sum(
            jnp.where(diagonal(), level[start : start + HD, :], 0.0), axis=0, keepdims=True
        )
        levels = jnp.where(seat == (to + start) // HD, flat, levels)
    return levels


def stage_kernel(plan, place_ref, *refs):
    refs = list(refs)
    init, finish, extra = plan["init"], plan["finish"], plan["extra"]
    own, mate, carrier = plan["own"], plan["mate"], plan["carrier"]
    rows_too = carrier is not None or extra
    node_ref = refs.pop(0) if extra else None
    blocks = [refs.pop(0) for _ in plan["counts"]]
    own_pack = refs.pop(0)
    mate_pack = refs.pop(0) if mate or rows_too else None
    if extra:
        rim, row_pairs = refs.pop(0), refs.pop(0)
    if not init:
        refs = refs[2 * (own + mate + rows_too) :]
    packed = refs.pop(0) if finish else None
    if own:
        own_top, own_mixed = refs.pop(0), refs.pop(0)
    if mate:
        mate_top, mate_mixed = refs.pop(0), refs.pop(0)
    if rows_too:
        rows_top, rows_mixed = refs.pop(0), refs.pop(0)
    keys, values, raw_keys, raw_values, numbers = refs
    place = place_ref[0]
    mate_place = place + RUN - 2 * RUN * ((place // RUN) % 2)
    y, z = (place // RUN) % RING_Y, (place // (RING_Y * RUN)) * RUN + place % RUN
    size = plan["size"]
    bound = mate_place if mate else place
    ones = jnp.ones((TOK, HD), jnp.bfloat16)

    def span_of(slot):
        return pl.ds(pl.multiple_of(slot * TOK, TOK), TOK)

    slot, count = 0, jnp.int32(0)
    for block, amount in zip(blocks, plan["counts"]):
        for part in range(amount):
            dz, other = plan["offsets"][slot]
            far_y, far_z = (RING_Y - 1 - y) if other else y, (z + dz + RING_Z) % RING_Z
            number = (far_z // RUN) * (RING_Y * RUN) + far_y * RUN + far_z % RUN
            numbers[slot] = number
            key = block[part * TOK : (part + 1) * TOK, :HD]
            value = jnp.concatenate([block[part * TOK : (part + 1) * TOK, HD:], ones], axis=1)
            if carrier is not None:
                raw_keys[slot * TOK : (slot + 1) * TOK, :] = key
                raw_values[slot * TOK : (slot + 1) * TOK, :] = value
            keys[span_of(count), :] = key
            values[span_of(count), :] = value
            count = count + (number < bound).astype(jnp.int32)
            slot += 1
    if not (init and own):
        for more in range(size - 1):
            keys[span_of(count + more), :] = keys[:TOK, :]
            values[span_of(count + more), :] = jnp.zeros((TOK, 2 * HD), jnp.bfloat16)

    if rows_too:
        decode_query = jnp.concatenate(head_rows(own_pack) + head_rows(mate_pack), axis=0)
    if carrier is not None:
        own_reach, mate_reach = reach_of(own_pack), reach_of(mate_pack)
        lane = lax.broadcasted_iota(jnp.int32, (ROW, TOK), 1).astype(jnp.float32)

    def decode():
        allowed = []
        for slot in range(len(plan["offsets"])):
            base = (numbers[slot] * TOK).astype(jnp.float32)
            fits = []
            for reach in (own_reach, mate_reach):
                left = reach - base
                fits += [lane < jnp.concatenate([left, left], axis=1)] * GROUP
            allowed.append(jnp.concatenate(fits, axis=0))
        spans = [slice(i * TOK, (i + 1) * TOK) for i in range(len(plan["offsets"]))]
        attend(
            decode_query,
            [raw_keys[span, :] for span in spans],
            [raw_values[span, :] for span in spans],
            allowed,
            True,
            rows_top,
            rows_mixed,
            slice(0, 2 * GROUP * ROW),
        )

    def prefill(pack, some_keys, some_values, allowed, top_ref, mixed_ref, at_once, active=None):
        def some_heads(turn, carry):
            for number in range(at_once):
                head = turn * at_once + number
                lanes = pl.ds(pl.multiple_of(head * HD, HD), HD)
                attend(
                    pack[pl.ds(0, TOK), lanes],
                    some_keys,
                    some_values,
                    allowed,
                    False,
                    top_ref,
                    mixed_ref,
                    pl.ds(pl.multiple_of(head * TOK, TOK), TOK),
                    active,
                )
            return carry

        if at_once == GROUP:
            some_heads(0, 0)
        else:
            lax.fori_loop(0, GROUP // at_once, some_heads, 0)

    fresh = [(own_top, own_mixed)] if init and own else []
    fresh += [(mate_top, mate_mixed), (rows_top, rows_mixed)] if init and mate else []
    for top_ref, mixed_ref in fresh:
        top_ref[...] = jnp.full(top_ref.shape, LOWEST, jnp.float32)
        mixed_ref[...] = jnp.zeros(mixed_ref.shape, jnp.float32)
    if init and own:
        token = lax.broadcasted_iota(jnp.int32, (TOK, TOK), 0)
        causal = [lax.broadcasted_iota(jnp.int32, (TOK, TOK), 1) <= token]
        prefill(own_pack, [keys[:TOK, :]], [values[:TOK, :]], causal, own_top, own_mixed, 4)
    else:
        pack = mate_pack if mate else own_pack
        top_ref, mixed_ref = (mate_top, mate_mixed) if mate else (own_top, own_mixed)

        def turn(number, carry, active=None):
            spans = [span_of(number * size + i) for i in range(size)]
            some_keys = [keys[span, :] for span in spans]
            some_values = [values[span, :] for span in spans]
            at_once = plan["at_once"]
            prefill(pack, some_keys, some_values, None, top_ref, mixed_ref, at_once, active)
            return carry

        if carrier is None:
            lax.fori_loop(0, (count + size - 1) // size, turn, 0)
        else:
            turn(0, 0, count > 0)
            decode()

    if extra:
        nodes = per_row(node_ref, place * ROW)
        seat = lax.broadcasted_iota(jnp.int32, (ROW, HD), 0)
        column = lax.broadcasted_iota(jnp.int32, (ROW, HD), 1)
        key_nodes = jnp.full((ROW, HD), -1, jnp.int32)
        previous = jnp.maximum(place - 1, 0) * ROW
        for row in range(ROW):
            rim_node = jnp.where(place > 0, node_ref[previous + row], -1)
            key_nodes = jnp.where(column == row, rim_node, key_nodes)
            key_nodes = jnp.where(column == ROW + row, node_ref[place * ROW + row], key_nodes)
        same = (key_nodes == nodes) & (column <= seat + ROW)
        pad = jnp.zeros((HD - 2 * ROW, HD), jnp.bfloat16)
        extra_ones = jnp.ones((HD, HD), jnp.bfloat16)
        extra_keys = jnp.concatenate([rim[:, :HD], row_pairs[:, :HD], pad], axis=0)
        extra_values = jnp.concatenate([rim[:, HD:], row_pairs[:, HD:], pad], axis=0)
        attend(
            decode_query[: GROUP * ROW],
            [extra_keys],
            [jnp.concatenate([extra_values, extra_ones], axis=1)],
            [jnp.concatenate([same] * GROUP, axis=0)],
            True,
            rows_top,
            rows_mixed,
            slice(0, GROUP * ROW),
        )

    if finish:
        levels = jnp.zeros((LEVELS, HD), jnp.float32)
        for head in range(GROUP):
            levels = seal(mate_top, mate_mixed, head * TOK, TOK, head * TOK, packed, levels)
        levels = seal(rows_top, rows_mixed, GROUP * ROW, HD, GROUP * TOK, packed, levels)
        for part in range(3):
            rounded = levels.astype(jnp.bfloat16)
            begin = HEIGHT + part * LEVELS
            packed[begin : begin + LEVELS, :] = rounded
            levels = levels - rounded.astype(jnp.float32)


def stage(
    place,
    packs,
    blocks,
    offsets,
    state,
    init=False,
    own=False,
    mate=False,
    carrier=None,
    finish=False,
    extra=None,
    at_once=4,
    size=5,
):
    rows_too = carrier is not None or extra is not None
    plan = dict(
        counts=[block.shape[0] // TOK for block in blocks],
        offsets=offsets,
        init=init,
        own=own,
        mate=mate,
        carrier=carrier,
        finish=finish,
        extra=extra is not None,
        at_once=at_once,
        size=size,
    )
    total = len(offsets)
    smem = [place] + ([extra[0]] if extra else [])
    packs = list(packs) if mate or rows_too else [packs[0]]
    operands = smem + list(blocks) + packs + (list(extra[1:]) if extra else [])
    used = [name for name, flag in (("own", own), ("mate", mate), ("rows", rows_too)) if flag]
    sizes = dict(own=GROUP * TOK, mate=GROUP * TOK, rows=2 * GROUP * ROW)
    shapes = [jax.ShapeDtypeStruct((HEIGHT + 3 * LEVELS, HD), jnp.bfloat16)] if finish else []
    aliases = {}
    for name in used:
        for index, width in enumerate((HD, 2 * HD)):
            if not init:
                aliases[len(operands)] = len(shapes)
                operands.append(state[name][index])
            shapes.append(jax.ShapeDtypeStruct((sizes[name], width), jnp.float32))
    work = total * TOK * TOK * GROUP * (own + mate)
    results = pl.pallas_call(
        functools.partial(stage_kernel, plan),
        in_specs=[IN_SMEM] * len(smem) + [IN_VMEM] * (len(operands) - len(smem)),
        out_specs=[IN_VMEM] * len(shapes),
        out_shape=shapes,
        scratch_shapes=[
            pltpu.VMEM(((total + size) * TOK, HD), jnp.bfloat16),
            pltpu.VMEM(((total + size) * TOK, 2 * HD), jnp.bfloat16),
            pltpu.VMEM((total * TOK, HD), jnp.bfloat16),
            pltpu.VMEM((total * TOK, 2 * HD), jnp.bfloat16),
            pltpu.SMEM((16,), jnp.int32),
        ],
        input_output_aliases=aliases,
        compiler_params=pltpu.CompilerParams(vmem_limit_bytes=VMEM),
        cost_estimate=pl.CostEstimate(
            flops=work * 8 * HD, bytes_accessed=2000000, transcendentals=work
        ),
    )(*operands)
    results = list(results)
    packed = results.pop(0) if finish else None
    state = dict(state or {})
    for name in used:
        state[name] = (results.pop(0), results.pop(0))
    return (state, packed) if finish else state


def merge_kernel(own_top, own_mixed, rows_top, rows_mixed, packed, out, out_rows):
    levels = jnp.zeros((LEVELS, HD), jnp.float32)
    for part in range(3):
        begin = HEIGHT + part * LEVELS
        levels = levels + packed[begin : begin + LEVELS, :].astype(jnp.float32)

    def joined(top_ref, mixed_ref, begin, at):
        rows = slice(begin, begin + HD)
        flat = levels[at // HD : at // HD + 1, :]
        level = jnp.sum(jnp.where(diagonal(), flat, 0.0), axis=1, keepdims=True)
        top = top_ref[rows, :]
        highest = jnp.maximum(top, level)
        mine, theirs = jnp.exp2(top - highest), jnp.exp2(level - highest)
        mixed = mixed_ref[rows, :]
        other = packed[at : at + HD, :].astype(jnp.float32)
        amount = mine * mixed[:, HD:] + theirs
        return ((mine * mixed[:, :HD] + theirs * other) / amount).astype(jnp.bfloat16)

    for head in range(GROUP):
        for start in range(0, TOK, HD):
            begin = head * TOK + start
            part = joined(own_top, own_mixed, begin, begin)
            out[start : start + HD, head * HD : (head + 1) * HD] = part
    part = joined(rows_top, rows_mixed, 0, GROUP * TOK)
    for head in range(GROUP):
        out_rows[:, head * HD : (head + 1) * HD] = part[head * ROW : (head + 1) * ROW, :]


def merge(state, packed):
    return pl.pallas_call(
        merge_kernel,
        in_specs=[IN_VMEM] * 5,
        out_specs=[IN_VMEM] * 2,
        out_shape=[
            jax.ShapeDtypeStruct((TOK, GROUP * HD), jnp.bfloat16),
            jax.ShapeDtypeStruct((ROW, GROUP * HD), jnp.bfloat16),
        ],
        compiler_params=pltpu.CompilerParams(vmem_limit_bytes=VMEM),
    )(*state["own"], *state["rows"], packed)


def per_device(
    hidden_context,
    hidden_rows,
    norm_gain,
    key_value_weight,
    value_bias,
    query_context,
    query_rows,
    context_length,
    row_node,
):
    weights = key_value_weight.reshape(D, 2 * HD)
    gain = norm_gain.reshape(8, WIDE)
    bias = value_bias.reshape(1, HD)
    tp = lax.axis_index("tp").astype(jnp.int32).reshape(1)
    place = lax.axis_index(PLACE).astype(jnp.int32).reshape(1)

    def swap(block, bits):
        return lax.ppermute(block, PLACE, [(i, i ^ bits) for i in range(32)])

    own = jnp.concatenate([hidden_context, hidden_rows], axis=0)
    low, high, twin = move_x(own, 1), move_x(own, -1), swap_core(own)
    digits = jnp.stack([context_length // 64, context_length % 64], axis=1)
    coded = jnp.repeat(digits.astype(jnp.bfloat16), HD, axis=1)
    coded = jnp.pad(coded, ((0, 0), (0, WIDE - 2 * HD)))
    own_pack = jnp.concatenate([query_context, query_rows, coded], axis=0)
    add = functools.partial(project, tp, gain)
    state = add(
        [[(hidden_context, 0, TOK), (hidden_rows, 0, ROW)], [(twin, 0, BOTH)]],
        [(0, 0), (0, 1)],
        weights,
    )
    low, high, state, own_pack = lax.optimization_barrier((low, high, state, own_pack))
    mate_pack = swap(own_pack, RUN)
    far_low, far_high = move_x(low[:TOP], 1), move_x(high[TOP:], -1)
    low_twin, high_twin = swap_core(low), swap_core(high)
    state, rest = add(
        [[(piece, 0, BOTH)] for piece in (low, high, low_twin, high_twin)],
        [(-1, 0), (1, 0), (-1, 1), (1, 1)],
        weights,
        later=[(2, 0), (2, 1)],
        state=state,
    )
    far_low, far_high, state, rest = lax.optimization_barrier((far_low, far_high, state, rest))
    far_twin = swap_core(jnp.concatenate([far_low, far_high], axis=0))
    far = [(far_low, 0, TOP), (far_high, 0, BOTH - TOP)]
    state = add([far], [(2, 0)], rest, held=[0], state=state)
    pairs, row_pairs = add(
        [[(far_twin, 0, BOTH)]], [(2, 1)], rest, held=[1], state=state, bias=bias
    )

    opposite = 3 * RUN
    run = functools.partial(stage, place, (own_pack, mate_pack))
    above, below = move(pairs, 1, 0), move(pairs, -1, 0)
    state = run([pairs], [(0, 0)], None, init=True, own=True)
    rim = lax.ppermute(row_pairs, PLACE, [(i, i + 1) for i in range(31)])
    above, below, state, rim = lax.optimization_barrier((above, below, state, rim))
    above_two, below_two = move(above, 1, 0), move(below, -1, 0)
    first = swap(jnp.concatenate([pairs, above, below], axis=0), opposite)
    above_two, below_two, mate_pack = lax.optimization_barrier((above_two, below_two, mate_pack))
    run = functools.partial(stage, place, (own_pack, mate_pack))
    above_three, below_three = move(above_two, 1, 0), move(below_two, -1, 0)
    second = swap(jnp.concatenate([above_two, below_two], axis=0), opposite)
    line = [pairs, above, below, above_two, below_two]
    steps = [(0, 0), (-1, 0), (1, 0), (-2, 0), (2, 0)]
    state = run(line, steps, state, init=True, mate=True, carrier="mate")
    above_three, below_three, state = lax.optimization_barrier((above_three, below_three, state))
    ends = [move(above_three[:TOP], 1, 0), move(below_three[TOP:], -1, 0)]
    third = swap(jnp.concatenate([above_three, below_three], axis=0), opposite)
    across = [first, second]
    across_steps = [(0, 1), (-1, 1), (1, 1), (-2, 1), (2, 1)]
    state = run(across, across_steps, state, mate=True, carrier="mate", at_once=GROUP)
    ends, state = lax.optimization_barrier((ends, state))
    end = jnp.concatenate(ends, axis=0)
    fourth = swap(end, opposite)
    late, late_steps = [above_three, below_three, end], [(-3, 0), (3, 0), (4, 0)]
    state = run(late, late_steps, state, mate=True, carrier="mate", size=3)
    last, last_steps = [third, fourth], [(-3, 1), (3, 1), (4, 1)]
    state, packed = run(last, last_steps, state, mate=True, carrier="mate", finish=True, size=3)
    sent = swap(packed, RUN)
    packed, state = lax.optimization_barrier((packed, state))
    state = run(
        line[1:] + across + late + last,
        steps[1:] + across_steps + late_steps + last_steps,
        state,
        own=True,
        extra=(row_node, rim, row_pairs),
        at_once=GROUP,
    )
    out, out_rows = merge(state, sent)
    return out, out_rows


def solution(mesh):
    return jax.shard_map(
        per_device,
        mesh=mesh,
        in_specs=(
            P(PLACE, "tp"),
            P(PLACE, "tp"),
            P(),
            P(None, None, "tp"),
            P("tp"),
            P(PLACE, "tp"),
            P(PLACE, "tp"),
            P(PLACE),
            P(),
        ),
        out_specs=(P(PLACE, "tp"), P(PLACE, "tp")),
        check_vma=False,
    )
```

profile of v0, /device:TPU:240, one launch (start us, length us, event | category | flops | bytes accessed | tf_op | source)
XLA Modules:
  0.0 97.8 jit_solution(16541840087391593030)
XLA Ops:
  0.6 1.1 %constant_dynamic-update-slice_fusion.1 = bf16[272,1024]{1,0:T(8,128)(2,1)S(1)} fusion(bf16[256,1024]{1,0:T(8,128)(2,1)} %refs_0_.2), kind=kLoop, calls=%fused_computation.9 | loop fusion | bytes 1048576
  1.7 0.8 constant_dynamic-update-slice_fusion
  2.5 0.0 collective-permute-start.2
  2.5 2.8 %collective-permute-start.1 = (bf16[272,1024]{1,0:T(8,128)(2,1)S(1)}, bf16[272,1024]{1,0:T(8,128)(2,1)S(1)}, u32[]{:S(2)}, u32[]{:S(2)}) collective-permute-start(bf16[272,1024]{1,0:T(8,128)(2,1)S(1)} %constant_dynamic-update-slice_fusion), channel_id=1, source_target_pairs={{0,6},{1,7},{2,0},{3,1},{4,2},{5,3},{6,4},{7,5},{8,14},{9,15},{10,... | collective-permute-start | bytes 1671176 | tf_op jit(solution)/shard_map/ppermute | solution.py:49
  5.2 0.0 collective-permute-start
  5.3 0.7 convert_bitcast_fusion
  5.9 0.1 copy.27
  6.0 0.1 broadcast_in_dim.3
  6.2 0.0 copy-start.4
  6.2 0.0 copy-start.5
  6.2 2.8 %copy.32 = bf16[1024,8,2,128]{3,1,2,0:T(8,128)(2,1)S(1)} copy(bf16[1024,8,2,128]{3,2,1,0:T(2,128)(2,1)} %bitcast.18) | data formatting | bytes 8388608
  9.0 0.0 copy-start
  9.0 0.0 copy-start.1
  9.1 0.0 collective-permute-done.2.refs_2_
  9.1 0.9 copy-done
  10.0 2.0 %shard_map.104 = (f32[272,256]{1,0:T(8,128)S(1)}, f32[272,128]{1,0:T(8,128)S(1)}) custom-call(s32[1]{0:T(128)} %bitcast.1.tp_ref, bf16[256,1024]{1,0:T(8,128)(2,1)S(1)} %copy-done, bf16[16,1024]{1,0:T(8,128)(2,1)S(1)} %copy-done.1, bf16[272,1024]{1,0:T(8,128)(2,1)S(1)} %collective-permute-done.2.refs_2_, bf16[8192,256]{1,0:T(8,128)(2,1)S(1)} %bitcast.15, ...), custom_call_target="tpu_custom_call" | custom-call | flops 285212672 | bytes 2200000 | tf_op jit(solution)/shard_map/pallas_call | solution.py:152
  12.0 5.8 %collective-permute-done.1.refs_1_ = bf16[272,1024]{1,0:T(8,128)(2,1)S(1)} collective-permute-done((bf16[272,1024]{1,0:T(8,128)(2,1)S(1)}, bf16[272,1024]{1,0:T(8,128)(2,1)S(1)}, u32[]{:S(2)}, u32[]{:S(2)}) %collective-permute-start.1) | collective-permute-done | bytes 557088 | tf_op jit(solution)/shard_map/ppermute | solution.py:49
  17.8 3.4 %collective-permute-done.refs_0_ = bf16[272,1024]{1,0:T(8,128)(2,1)S(1)} collective-permute-done((bf16[272,1024]{1,0:T(8,128)(2,1)S(1)}, bf16[272,1024]{1,0:T(8,128)(2,1)S(1)}, u32[]{:S(2)}, u32[]{:S(2)}) %collective-permute-start) | collective-permute-done | bytes 557088 | tf_op jit(solution)/shard_map/ppermute | solution.py:49
  21.2 0.0 collective-permute-start.5
  21.2 0.5 collective-permute-start.6
  21.8 0.4 collective-permute-start.4
  22.1 1.8 %collective-permute-start.3 = (bf16[128,1024]{1,0:T(8,128)(2,1)S(1)}, bf16[128,1024]{1,0:T(8,128)(2,1)S(1)}, u32[]{:S(2)}, u32[]{:S(2)}) collective-permute-start(bf16[128,1024]{1,0:T(8,128)(2,1)S(1)} %slice.12), channel_id=1, source_target_pairs={{0,2},{1,3},{2,4},{3,5},{4,6},{5,7},{6,0},{7,1},{8,10},{9,11},{10,... | collective-permute-start | bytes 786440 | tf_op jit(solution)/shard_map/ppermute | solution.py:49
  24.0 0.0 collective-permute-done.5.refs_2_
  24.0 0.0 collective-permute-done.6.refs_3_
  24.0 4.2 %shard_map.105 = (f32[272,256]{1,0:T(8,128)S(1)}, f32[272,128]{1,0:T(8,128)S(1)}, bf16[2,1024,256]{2,1,0:T(8,128)(2,1)S(1)}) custom-call(s32[1]{0:T(128)} %bitcast.1.tp_ref, bf16[272,1024]{1,0:T(8,128)(2,1)S(1)} %collective-permute-done.refs_0_, bf16[272,1024]{1,0:T(8,128)(2,1)S(1)} %collective-permute-done.1.refs_1_, ...), custom_call_target="tpu_custom_call" | custom-call | flops 570425344 | bytes 4400000 | tf_op jit(solution)/shard_map/pallas_call | solution.py:152
  28.1 3.2 %collective-permute-done.3.refs_0_ = bf16[128,1024]{1,0:T(8,128)(2,1)S(1)} collective-permute-done((bf16[128,1024]{1,0:T(8,128)(2,1)S(1)}, bf16[128,1024]{1,0:T(8,128)(2,1)S(1)}, u32[]{:S(2)}, u32[]{:S(2)}) %collective-permute-start.3) | collective-permute-done | bytes 262176 | tf_op jit(solution)/shard_map/ppermute | solution.py:49
  31.4 0.0 collective-permute-done.4.refs_1_
  31.4 0.0 copy-start.2
  31.4 0.1 collective-permute-start.7
  31.5 1.4 %collective-permute-start.13 = (bf16[288,1024]{1,0:T(8,128)(2,1)S(1)}, bf16[288,1024]{1,0:T(8,128)(2,1)S(1)}, u32[]{:S(2)}, u32[]{:S(2)}) collective-permute-start(bf16[288,1024]{1,0:T(8,128)(2,1)S(1)} %fusion.1.refs_1_.refs_5_.refs_2_.refs_3_.refs_12_), channel_id=1, source_target_pairs={{0,32},{8,40},{16,48},{24,56},{32,0},{40,8},{48,16},{56,24},{64,96... | collective-permute-start | bytes 1769480 | tf_op jit(solution)/shard_map/ppermute | solution.py:537
  32.9 0.3 shard_map.106
  33.3 0.2 collective-permute-done.7.refs_0_
  33.5 0.3 shard_map.107
  33.8 1.1 %collective-permute-start.9 = (bf16[256,256]{1,0:T(8,128)(2,1)S(1)}, bf16[256,256]{1,0:T(8,128)(2,1)S(1)}, u32[]{:S(2)}, u32[]{:S(2)}) collective-permute-start(bf16[256,256]{1,0:T(8,128)(2,1)S(1)} %get-tuple-element.86.refs_0_), channel_id=1, source_target_pairs={{0,152},{8,0},{16,8},{24,16},{128,24},{136,128},{144,136},{152,144... | collective-permute-start | bytes 393224 | tf_op jit(solution)/shard_map/ppermute | solution.py:45
  34.9 2.2 %collective-permute-start.8 = (bf16[256,256]{1,0:T(8,128)(2,1)S(1)}, bf16[256,256]{1,0:T(8,128)(2,1)S(1)}, u32[]{:S(2)}, u32[]{:S(2)}) collective-permute-start(bf16[256,256]{1,0:T(8,128)(2,1)S(1)} %get-tuple-element.86.refs_0_), channel_id=1, source_target_pairs={{0,8},{8,16},{16,24},{24,128},{128,136},{136,144},{144,152},{152,0... | collective-permute-start | bytes 393224 | tf_op jit(solution)/shard_map/ppermute | solution.py:45
  37.1 3.3 %collective-permute-start.10 = (bf16[16,256]{1,0:T(8,128)(2,1)S(1)}, bf16[16,256]{1,0:T(8,128)(2,1)S(1)}, u32[]{:S(2)}, u32[]{:S(2)}) collective-permute-start(bf16[16,256]{1,0:T(8,128)(2,1)S(1)} %get-tuple-element.90.refs_15_), channel_id=1, source_target_pairs={{0,8},{8,16},{16,24},{24,32},{32,40},{40,48},{48,56},{56,64},{64,7... | collective-permute-start | bytes 24584 | tf_op jit(solution)/shard_map/ppermute | solution.py:574
  40.5 1.6 %shard_map.108 = (f32[2048,128]{1,0:T(8,128)S(1)}, f32[2048,256]{1,0:T(8,128)S(1)}) custom-call(s32[1]{0:T(128)} %bitcast.place_ref, bf16[256,256]{1,0:T(8,128)(2,1)S(1)} %get-tuple-element.86.refs_0_, bf16[288,1024]{1,0:T(8,128)(2,1)S(1)} %fusion.1.refs_1_.refs_5_.refs_2_.refs_3_.refs_12_), custom_call_target="tpu_custom_call" | custom-call | flops 536870912 | bytes 2000000 | tf_op jit(solution)/shard_map/pallas_call | solution.py:452
  42.0 0.7 collective-permute-done.10.refs_14_
  42.7 0.0 collective-permute-done.9.refs_2_
  42.7 2.7 %collective-permute-start.11 = (bf16[256,256]{1,0:T(8,128)(2,1)S(1)}, bf16[256,256]{1,0:T(8,128)(2,1)S(1)}, u32[]{:S(2)}, u32[]{:S(2)}) collective-permute-start(bf16[256,256]{1,0:T(8,128)(2,1)S(1)} %collective-permute-done.8.refs_1_), channel_id=1, source_target_pairs={{0,8},{8,16},{16,24},{24,128},{128,136},{136,144},{144,152},{152,0... | collective-permute-start | bytes 393224 | tf_op jit(solution)/shard_map/ppermute | solution.py:45
  45.4 0.0 collective-permute-start.12
  45.4 0.6 collective-permute-start.14
  46.1 1.2 %collective-permute-done.13.refs_6_.refs_3_.refs_4_.refs_13_ = bf16[288,1024]{1,0:T(8,128)(2,1)S(1)} collective-permute-done((bf16[288,1024]{1,0:T(8,128)(2,1)S(1)}, bf16[288,1024]{1,0:T(8,128)(2,1)S(1)}, u32[]{:S(2)}, u32[]{:S(2)}) %collective-permute-start.13) | collective-permute-done | bytes 589856 | tf_op jit(solution)/shard_map/ppermute | solution.py:537
  47.3 0.6 collective-permute-done.11.refs_3_
  47.9 3.7 %collective-permute-done.12.refs_4_ = bf16[256,256]{1,0:T(8,128)(2,1)S(1)} collective-permute-done((bf16[256,256]{1,0:T(8,128)(2,1)S(1)}, bf16[256,256]{1,0:T(8,128)(2,1)S(1)}, u32[]{:S(2)}, u32[]{:S(2)}) %collective-permute-start.12) | collective-permute-done | bytes 131104 | tf_op jit(solution)/shard_map/ppermute | solution.py:45
  51.6 0.0 collective-permute-start.16
  51.6 2.0 %collective-permute-start.17 = (bf16[256,256]{1,0:T(8,128)(2,1)S(1)}, bf16[256,256]{1,0:T(8,128)(2,1)S(1)}, u32[]{:S(2)}, u32[]{:S(2)}) collective-permute-start(bf16[256,256]{1,0:T(8,128)(2,1)S(1)} %collective-permute-done.12.refs_4_), channel_id=1, source_target_pairs={{0,152},{8,0},{16,8},{24,16},{128,24},{136,128},{144,136},{152,144... | collective-permute-start | bytes 393224 | tf_op jit(solution)/shard_map/ppermute | solution.py:45
  53.6 0.6 collective-permute-start.15
  54.3 5.9 %shard_map.109 = (f32[2048,128]{1,0:T(8,128)S(1)}, f32[2048,256]{1,0:T(8,128)S(1)}, f32[256,128]{1,0:T(8,128)S(1)}, f32[256,256]{1,0:T(8,128)S(1)}) custom-call(s32[1]{0:T(128)} %bitcast.place_ref, bf16[256,256]{1,0:T(8,128)(2,1)S(1)} %get-tuple-element.86.refs_0_, bf16[256,256]{1,0:T(8,128)(2,1)S(1)} %collective-permute-done.8.refs_1_, ...), custom_call_target="tpu_custom_call" | custom-call | flops 2684354560 | bytes 2000000 | tf_op jit(solution)/shard_map/pallas_call | solution.py:452
  60.2 0.0 collective-permute-done.16.refs_0_.refs_7_
  60.3 0.1 collective-permute-start.19
  60.3 3.2 %collective-permute-start.18 = (bf16[128,256]{1,0:T(8,128)(2,1)S(1)}, bf16[128,256]{1,0:T(8,128)(2,1)S(1)}, u32[]{:S(2)}, u32[]{:S(2)}) collective-permute-start(bf16[128,256]{1,0:T(8,128)(2,1)S(1)} %slice.14), channel_id=1, source_target_pairs={{0,8},{8,16},{16,24},{24,128},{128,136},{136,144},{144,152},{152,0... | collective-permute-start | bytes 196616 | tf_op jit(solution)/shard_map/ppermute | solution.py:45
  63.6 1.8 %collective-permute-start.20 = (bf16[512,256]{1,0:T(8,128)(2,1)S(1)}, bf16[512,256]{1,0:T(8,128)(2,1)S(1)}, u32[]{:S(2)}, u32[]{:S(2)}) collective-permute-start(bf16[512,256]{1,0:T(8,128)(2,1)S(1)} %pad_maximum_fusion.3), channel_id=1, source_target_pairs={{0,96},{8,104},{16,112},{24,120},{32,64},{40,72},{48,80},{56,88},{... | collective-permute-start | bytes 786440 | tf_op jit(solution)/shard_map/ppermute | solution.py:537
  65.4 4.5 %shard_map.110 = (f32[2048,128]{1,0:T(8,128)S(1)}, f32[2048,256]{1,0:T(8,128)S(1)}, f32[256,128]{1,0:T(8,128)S(1)}, f32[256,256]{1,0:T(8,128)S(1)}) custom-call(s32[1]{0:T(128)} %bitcast.place_ref, bf16[768,256]{1,0:T(8,128)(2,1)S(1)} %collective-permute-done.14.refs_0_.refs_5_, ...), custom_call_target="tpu_custom_call", output_to_operand_aliasing={{0}: (5, {}), {1}: (6, {}), {2}: (7, {}), {3}: (8, {})} | custom-call | flops 2684354560 | bytes 2000000 | tf_op jit(solution)/shard_map/pallas_call | solution.py:452
  69.9 0.0 collective-permute-done.19
  69.9 0.0 collective-permute-done.18
  69.9 0.6 collective-permute-start.21
  70.6 3.7 %shard_map.111 = (f32[2048,128]{1,0:T(8,128)S(1)}, f32[2048,256]{1,0:T(8,128)S(1)}, f32[256,128]{1,0:T(8,128)S(1)}, f32[256,256]{1,0:T(8,128)S(1)}) custom-call(s32[1]{0:T(128)} %bitcast.place_ref, bf16[256,256]{1,0:T(8,128)(2,1)S(1)} %collective-permute-done.16.refs_0_.refs_7_, ...), custom_call_target="tpu_custom_call", output_to_operand_aliasing={{0}: (6, {}), {1}: (7, {}), {2}: (8, {}), {3}: (9, {})} | custom-call | flops 1610612736 | bytes 2000000 | tf_op jit(solution)/shard_map/pallas_call | solution.py:452
  74.3 0.7 collective-permute-done.21.refs_1_.refs_11_
  75.0 4.1 %shard_map.112 = (bf16[2272,128]{1,0:T(8,128)(2,1)S(1)}, f32[2048,128]{1,0:T(8,128)S(1)}, f32[2048,256]{1,0:T(8,128)S(1)}, f32[256,128]{1,0:T(8,128)S(1)}, f32[256,256]{1,0:T(8,128)S(1)}) custom-call(s32[1]{0:T(128)} %bitcast.place_ref, ...), custom_call_target="tpu_custom_call", output_to_operand_aliasing={{1}: (5, {}), {2}: (6, {}), {3}: (7, {}), {4}: (8, {})} | custom-call | flops 1610612736 | bytes 2000000 | tf_op jit(solution)/shard_map/pallas_call | solution.py:452
  79.1 3.8 %collective-permute-start.22 = (bf16[2272,128]{1,0:T(8,128)(2,1)S(1)}, bf16[2272,128]{1,0:T(8,128)(2,1)S(1)}, u32[]{:S(2)}, u32[]{:S(2)}) collective-permute-start(bf16[2272,128]{1,0:T(8,128)(2,1)S(1)} %get-tuple-element.125), channel_id=1, source_target_pairs={{0,32},{8,40},{16,48},{24,56},{32,0},{40,8},{48,16},{56,24},{64,96... | collective-permute-start | bytes 1744904 | tf_op jit(solution)/shard_map/ppermute | solution.py:537
  82.8 13.5 %shard_map.113 = (f32[2048,128]{1,0:T(8,128)S(1)}, f32[2048,256]{1,0:T(8,128)S(1)}, f32[256,128]{1,0:T(8,128)S(1)}, f32[256,256]{1,0:T(8,128)S(1)}) custom-call(s32[1]{0:T(128)} %bitcast.place_ref, s32[512]{0:T(512)S(1)} %copy-done.3, ...), custom_call_target="tpu_custom_call", output_to_operand_aliasing={{0}: (17, {}), {1}: (18, {}), {2}: (19, {}), {3}: (20, {})} | custom-call | flops 8053063680 | bytes 2000000 | tf_op jit(solution)/shard_map/pallas_call | solution.py:452
  96.4 0.0 collective-permute-done.22.packed
  96.4 1.4 %shard_map.114 = (bf16[256,1024]{1,0:T(8,128)(2,1)}, bf16[16,1024]{1,0:T(8,128)(2,1)}) custom-call(f32[2048,128]{1,0:T(8,128)S(1)} %get-tuple-element.134.own_top, f32[2048,256]{1,0:T(8,128)S(1)} %get-tuple-element.135.own_mixed, f32[256,128]{1,0:T(8,128)S(1)} %get-tuple-element.136.rows_top, f32[256,256]{1,0:T(8,128)S(1)} %get-tuple-element.137.rows_mixed, ...), custom_call_target="tpu_custom_call" | custom-call | tf_op jit(solution)/shard_map/pallas_call | solution.py:507
  (27 shorter events, 0.3 us)
Async XLA Ops:
  0.6 5.5 %copy-start.6 = (f32[8192]{0:T(1024)S(1)}, f32[8192]{0:T(1024)}, u32[]{:S(2)}) copy-start(f32[8192]{0:T(1024)} %param.11) | copy-start | bytes 98308
  2.5 6.6 %collective-permute-start.2 = (bf16[272,1024]{1,0:T(8,128)(2,1)S(1)}, bf16[272,1024]{1,0:T(8,128)(2,1)S(1)}, u32[]{:S(2)}, u32[]{:S(2)}) collective-permute-start(bf16[272,1024]{1,0:T(8,128)(2,1)S(1)} %constant_dynamic-update-slice_fusion), channel_id=1, source_target_pairs={{0,1},{1,0},{2,3},{3,2},{4,5},{5,4},{6,7},{7,6},{8,9},{9,8},{10,11... | collective-permute-start | bytes 1671176 | tf_op jit(solution)/shard_map/ppermute | solution.py:53
  2.5 15.3 %collective-permute-start.1 = (bf16[272,1024]{1,0:T(8,128)(2,1)S(1)}, bf16[272,1024]{1,0:T(8,128)(2,1)S(1)}, u32[]{:S(2)}, u32[]{:S(2)}) collective-permute-start(bf16[272,1024]{1,0:T(8,128)(2,1)S(1)} %constant_dynamic-update-slice_fusion), channel_id=1, source_target_pairs={{0,6},{1,7},{2,0},{3,1},{4,2},{5,3},{6,4},{7,5},{8,14},{9,15},{10,... | collective-permute-start | bytes 1671176 | tf_op jit(solution)/shard_map/ppermute | solution.py:49
  5.2 16.0 %collective-permute-start = (bf16[272,1024]{1,0:T(8,128)(2,1)S(1)}, bf16[272,1024]{1,0:T(8,128)(2,1)S(1)}, u32[]{:S(2)}, u32[]{:S(2)}) collective-permute-start(bf16[272,1024]{1,0:T(8,128)(2,1)S(1)} %constant_dynamic-update-slice_fusion), channel_id=1, source_target_pairs={{0,2},{1,3},{2,4},{3,5},{4,6},{5,7},{6,0},{7,1},{8,10},{9,11},{10,... | collective-permute-start | bytes 1671176 | tf_op jit(solution)/shard_map/ppermute | solution.py:49
  6.2 2.8 %copy-start.4 = (bf16[256,1024]{1,0:T(8,128)(2,1)S(1)}, bf16[256,1024]{1,0:T(8,128)(2,1)}, u32[]{:S(2)}) copy-start(bf16[256,1024]{1,0:T(8,128)(2,1)} %param.14) | copy-start | bytes 1572868
  6.2 2.8 %copy-start.5 = (bf16[16,1024]{1,0:T(8,128)(2,1)S(1)}, bf16[16,1024]{1,0:T(8,128)(2,1)}, u32[]{:S(2)}) copy-start(bf16[16,1024]{1,0:T(8,128)(2,1)} %param.15) | copy-start | bytes 98308
  9.0 1.0 %copy-start = (bf16[256,1024]{1,0:T(8,128)(2,1)S(1)}, bf16[256,1024]{1,0:T(8,128)(2,1)}, u32[]{:S(2)}) copy-start(bf16[256,1024]{1,0:T(8,128)(2,1)} %refs_0_.2) | copy-start | bytes 1572868
  9.0 1.0 %copy-start.1 = (bf16[16,1024]{1,0:T(8,128)(2,1)S(1)}, bf16[16,1024]{1,0:T(8,128)(2,1)}, u32[]{:S(2)}) copy-start(bf16[16,1024]{1,0:T(8,128)(2,1)} %refs_1_.1) | copy-start | bytes 98308
  21.2 2.7 %collective-permute-start.5 = (bf16[272,1024]{1,0:T(8,128)(2,1)S(1)}, bf16[272,1024]{1,0:T(8,128)(2,1)S(1)}, u32[]{:S(2)}, u32[]{:S(2)}) collective-permute-start(bf16[272,1024]{1,0:T(8,128)(2,1)S(1)} %collective-permute-done.refs_0_), channel_id=1, source_target_pairs={{0,1},{1,0},{2,3},{3,2},{4,5},{5,4},{6,7},{7,6},{8,9},{9,8},{10,11... | collective-permute-start | bytes 1671176 | tf_op jit(solution)/shard_map/ppermute | solution.py:53
  21.2 2.8 %collective-permute-start.6 = (bf16[272,1024]{1,0:T(8,128)(2,1)S(1)}, bf16[272,1024]{1,0:T(8,128)(2,1)S(1)}, u32[]{:S(2)}, u32[]{:S(2)}) collective-permute-start(bf16[272,1024]{1,0:T(8,128)(2,1)S(1)} %collective-permute-done.1.refs_1_), channel_id=1, source_target_pairs={{0,1},{1,0},{2,3},{3,2},{4,5},{5,4},{6,7},{7,6},{8,9},{9,8},{10,11... | collective-permute-start | bytes 1671176 | tf_op jit(solution)/shard_map/ppermute | solution.py:53
  21.8 9.6 %collective-permute-start.4 = (bf16[144,1024]{1,0:T(8,128)(2,1)S(1)}, bf16[144,1024]{1,0:T(8,128)(2,1)S(1)}, u32[]{:S(2)}, u32[]{:S(2)}) collective-permute-start(bf16[144,1024]{1,0:T(8,128)(2,1)S(1)} %slice.13), channel_id=1, source_target_pairs={{0,6},{1,7},{2,0},{3,1},{4,2},{5,3},{6,4},{7,5},{8,14},{9,15},{10,... | collective-permute-start | bytes 884744 | tf_op jit(solution)/shard_map/ppermute | solution.py:49
  22.1 9.2 %collective-permute-start.3 = (bf16[128,1024]{1,0:T(8,128)(2,1)S(1)}, bf16[128,1024]{1,0:T(8,128)(2,1)S(1)}, u32[]{:S(2)}, u32[]{:S(2)}) collective-permute-start(bf16[128,1024]{1,0:T(8,128)(2,1)S(1)} %slice.12), channel_id=1, source_target_pairs={{0,2},{1,3},{2,4},{3,5},{4,6},{5,7},{6,0},{7,1},{8,10},{9,11},{10,... | collective-permute-start | bytes 786440 | tf_op jit(solution)/shard_map/ppermute | solution.py:49
  31.4 2.1 %copy-start.2 = (f32[128]{0:T(128)S(1)}, f32[128]{0:T(128)}, u32[]{:S(2)}) copy-start(f32[128]{0:T(128)} %param.13) | copy-start | bytes 1540
  31.4 2.0 %collective-permute-start.7 = (bf16[272,1024]{1,0:T(8,128)(2,1)S(1)}, bf16[272,1024]{1,0:T(8,128)(2,1)S(1)}, u32[]{:S(2)}, u32[]{:S(2)}) collective-permute-start(bf16[272,1024]{1,0:T(8,128)(2,1)S(1)} %pad_maximum_fusion), channel_id=1, source_target_pairs={{0,1},{1,0},{2,3},{3,2},{4,5},{5,4},{6,7},{7,6},{8,9},{9,8},{10,11... | collective-permute-start | bytes 1671176 | tf_op jit(solution)/shard_map/ppermute | solution.py:53
  31.5 15.7 %collective-permute-start.13 = (bf16[288,1024]{1,0:T(8,128)(2,1)S(1)}, bf16[288,1024]{1,0:T(8,128)(2,1)S(1)}, u32[]{:S(2)}, u32[]{:S(2)}) collective-permute-start(bf16[288,1024]{1,0:T(8,128)(2,1)S(1)} %fusion.1.refs_1_.refs_5_.refs_2_.refs_3_.refs_12_), channel_id=1, source_target_pairs={{0,32},{8,40},{16,48},{24,56},{32,0},{40,8},{48,16},{56,24},{64,96... | collective-permute-start | bytes 1769480 | tf_op jit(solution)/shard_map/ppermute | solution.py:537
  33.8 8.8 %collective-permute-start.9 = (bf16[256,256]{1,0:T(8,128)(2,1)S(1)}, bf16[256,256]{1,0:T(8,128)(2,1)S(1)}, u32[]{:S(2)}, u32[]{:S(2)}) collective-permute-start(bf16[256,256]{1,0:T(8,128)(2,1)S(1)} %get-tuple-element.86.refs_0_), channel_id=1, source_target_pairs={{0,152},{8,0},{16,8},{24,16},{128,24},{136,128},{144,136},{152,144... | collective-permute-start | bytes 393224 | tf_op jit(solution)/shard_map/ppermute | solution.py:45
  34.9 7.8 %collective-permute-start.8 = (bf16[256,256]{1,0:T(8,128)(2,1)S(1)}, bf16[256,256]{1,0:T(8,128)(2,1)S(1)}, u32[]{:S(2)}, u32[]{:S(2)}) collective-permute-start(bf16[256,256]{1,0:T(8,128)(2,1)S(1)} %get-tuple-element.86.refs_0_), channel_id=1, source_target_pairs={{0,8},{8,16},{16,24},{24,128},{128,136},{136,144},{144,152},{152,0... | collective-permute-start | bytes 393224 | tf_op jit(solution)/shard_map/ppermute | solution.py:45
  37.1 5.5 %collective-permute-start.10 = (bf16[16,256]{1,0:T(8,128)(2,1)S(1)}, bf16[16,256]{1,0:T(8,128)(2,1)S(1)}, u32[]{:S(2)}, u32[]{:S(2)}) collective-permute-start(bf16[16,256]{1,0:T(8,128)(2,1)S(1)} %get-tuple-element.90.refs_15_), channel_id=1, source_target_pairs={{0,8},{8,16},{16,24},{24,32},{32,40},{40,48},{48,56},{56,64},{64,7... | collective-permute-start | bytes 24584 | tf_op jit(solution)/shard_map/ppermute | solution.py:574
  42.7 5.2 %collective-permute-start.11 = (bf16[256,256]{1,0:T(8,128)(2,1)S(1)}, bf16[256,256]{1,0:T(8,128)(2,1)S(1)}, u32[]{:S(2)}, u32[]{:S(2)}) collective-permute-start(bf16[256,256]{1,0:T(8,128)(2,1)S(1)} %collective-permute-done.8.refs_1_), channel_id=1, source_target_pairs={{0,8},{8,16},{16,24},{24,128},{128,136},{136,144},{144,152},{152,0... | collective-permute-start | bytes 393224 | tf_op jit(solution)/shard_map/ppermute | solution.py:45
  45.4 6.2 %collective-permute-start.12 = (bf16[256,256]{1,0:T(8,128)(2,1)S(1)}, bf16[256,256]{1,0:T(8,128)(2,1)S(1)}, u32[]{:S(2)}, u32[]{:S(2)}) collective-permute-start(bf16[256,256]{1,0:T(8,128)(2,1)S(1)} %collective-permute-done.9.refs_2_), channel_id=1, source_target_pairs={{0,152},{8,0},{16,8},{24,16},{128,24},{136,128},{144,136},{152,144... | collective-permute-start | bytes 393224 | tf_op jit(solution)/shard_map/ppermute | solution.py:45
  45.4 19.9 %collective-permute-start.14 = (bf16[768,256]{1,0:T(8,128)(2,1)S(1)}, bf16[768,256]{1,0:T(8,128)(2,1)S(1)}, u32[]{:S(2)}, u32[]{:S(2)}) collective-permute-start(bf16[768,256]{1,0:T(8,128)(2,1)S(1)} %pad_maximum_fusion.1), channel_id=1, source_target_pairs={{0,96},{8,104},{16,112},{24,120},{32,64},{40,72},{48,80},{56,88},{... | collective-permute-start | bytes 1179656 | tf_op jit(solution)/shard_map/ppermute | solution.py:537
  51.6 8.6 %collective-permute-start.16 = (bf16[256,256]{1,0:T(8,128)(2,1)S(1)}, bf16[256,256]{1,0:T(8,128)(2,1)S(1)}, u32[]{:S(2)}, u32[]{:S(2)}) collective-permute-start(bf16[256,256]{1,0:T(8,128)(2,1)S(1)} %collective-permute-done.11.refs_3_), channel_id=1, source_target_pairs={{0,8},{8,16},{16,24},{24,128},{128,136},{136,144},{144,152},{152,0... | collective-permute-start | bytes 393224 | tf_op jit(solution)/shard_map/ppermute | solution.py:45
  51.6 8.6 %collective-permute-start.17 = (bf16[256,256]{1,0:T(8,128)(2,1)S(1)}, bf16[256,256]{1,0:T(8,128)(2,1)S(1)}, u32[]{:S(2)}, u32[]{:S(2)}) collective-permute-start(bf16[256,256]{1,0:T(8,128)(2,1)S(1)} %collective-permute-done.12.refs_4_), channel_id=1, source_target_pairs={{0,152},{8,0},{16,8},{24,16},{128,24},{136,128},{144,136},{152,144... | collective-permute-start | bytes 393224 | tf_op jit(solution)/shard_map/ppermute | solution.py:45
  53.6 11.7 %collective-permute-start.15 = (bf16[512,256]{1,0:T(8,128)(2,1)S(1)}, bf16[512,256]{1,0:T(8,128)(2,1)S(1)}, u32[]{:S(2)}, u32[]{:S(2)}) collective-permute-start(bf16[512,256]{1,0:T(8,128)(2,1)S(1)} %pad_maximum_fusion.2), channel_id=1, source_target_pairs={{0,96},{8,104},{16,112},{24,120},{32,64},{40,72},{48,80},{56,88},{... | collective-permute-start | bytes 786440 | tf_op jit(solution)/shard_map/ppermute | solution.py:537
  60.3 9.6 %collective-permute-start.19 = (bf16[128,256]{1,0:T(8,128)(2,1)S(1)}, bf16[128,256]{1,0:T(8,128)(2,1)S(1)}, u32[]{:S(2)}, u32[]{:S(2)}) collective-permute-start(bf16[128,256]{1,0:T(8,128)(2,1)S(1)} %slice.15), channel_id=1, source_target_pairs={{0,152},{8,0},{16,8},{24,16},{128,24},{136,128},{144,136},{152,144... | collective-permute-start | bytes 196616 | tf_op jit(solution)/shard_map/ppermute | solution.py:45
  60.3 9.5 %collective-permute-start.18 = (bf16[128,256]{1,0:T(8,128)(2,1)S(1)}, bf16[128,256]{1,0:T(8,128)(2,1)S(1)}, u32[]{:S(2)}, u32[]{:S(2)}) collective-permute-start(bf16[128,256]{1,0:T(8,128)(2,1)S(1)} %slice.14), channel_id=1, source_target_pairs={{0,8},{8,16},{16,24},{24,128},{128,136},{136,144},{144,152},{152,0... | collective-permute-start | bytes 196616 | tf_op jit(solution)/shard_map/ppermute | solution.py:45
  63.6 11.4 %collective-permute-start.20 = (bf16[512,256]{1,0:T(8,128)(2,1)S(1)}, bf16[512,256]{1,0:T(8,128)(2,1)S(1)}, u32[]{:S(2)}, u32[]{:S(2)}) collective-permute-start(bf16[512,256]{1,0:T(8,128)(2,1)S(1)} %pad_maximum_fusion.3), channel_id=1, source_target_pairs={{0,96},{8,104},{16,112},{24,120},{32,64},{40,72},{48,80},{56,88},{... | collective-permute-start | bytes 786440 | tf_op jit(solution)/shard_map/ppermute | solution.py:537
  69.9 5.1 %collective-permute-start.21 = (bf16[256,256]{1,0:T(8,128)(2,1)S(1)}, bf16[256,256]{1,0:T(8,128)(2,1)S(1)}, u32[]{:S(2)}, u32[]{:S(2)}) collective-permute-start(bf16[256,256]{1,0:T(8,128)(2,1)S(1)} %constant_dynamic-update-slice_fusion.2.refs_2_.refs_9_), channel_id=1, source_target_pairs={{0,96},{8,104},{16,112},{24,120},{32,64},{40,72},{48,80},{56,88},{... | collective-permute-start | bytes 393224 | tf_op jit(solution)/shard_map/ppermute | solution.py:537
  75.0 7.9 %copy-start.3 = (s32[512]{0:T(512)S(1)}, s32[512]{0:T(512)}, u32[]{:S(2)}) copy-start(s32[512]{0:T(512)} %refs_0_.3) | copy-start | bytes 6148
  79.1 17.3 %collective-permute-start.22 = (bf16[2272,128]{1,0:T(8,128)(2,1)S(1)}, bf16[2272,128]{1,0:T(8,128)(2,1)S(1)}, u32[]{:S(2)}, u32[]{:S(2)}) collective-permute-start(bf16[2272,128]{1,0:T(8,128)(2,1)S(1)} %get-tuple-element.125), channel_id=1, source_target_pairs={{0,32},{8,40},{16,48},{24,56},{32,0},{40,8},{48,16},{56,24},{64,96... | collective-permute-start | bytes 1744904 | tf_op jit(solution)/shard_map/ppermute | solution.py:537
where the time goes:
time: 98 us; the launch traced here: 97.8 us
  Pallas kernels  41.6 us (42%)
  starting transfers between devices  29.1 us (30%)
  waiting for transfers between devices  19.5 us (20%)
  local copies, waits for them, and re-layouts  5.87 us (6%)
    pallas_call x6, Pallas kernels, stage(): pl.pallas_call(functools.partial(stage_kernel, plan), in_specs=[IN_SMEM]...  33.3 us
    ppermute x4, waiting for transfers between devices, move_x(): lax.ppermute(block, 'tp', [(i, (i + 2 * step) % 8) for i in range(8)])  12.4 us
    ppermute x8, starting transfers between devices, move(): return lax.ppermute(block, PLACE, route)  11.3 us
    ppermute x6, starting transfers between devices, swap(): return lax.ppermute(block, PLACE, [(i, i ^ bits) for i in range(32)])  8.87 us
    pallas_call x4, Pallas kernels, project(): pl.pallas_call(functools.partial(project_kernel, spans, shifts, later, he...  6.85 us
    ppermute x4, starting transfers between devices, move_x(): lax.ppermute(block, 'tp', [(i, (i + 2 * step) % 8) for i in range(8)])  4.94 us
    unnamed x18, local copies, waits for them, and re-layouts  4.86 us
    ppermute x8, waiting for transfers between devices, move(): return lax.ppermute(block, PLACE, route)  4.3 us
  transfers between devices with their start and end apart: 23, of which 9 were waited for; matrix products, arithmetic and copies ran while one was open for 4% of the time, Pallas kernels for 37%

commit v1 on v0

--- a/solution.py
+++ b/solution.py
@@ -259,7 +259,7 @@
         mate_top, mate_mixed = refs.pop(0), refs.pop(0)
     if rows_too:
         rows_top, rows_mixed = refs.pop(0), refs.pop(0)
-    keys, values, raw_keys, raw_values, numbers = refs
+    keys, values, decode_query, numbers = refs
     place = place_ref[0]
     mate_place = place + RUN - 2 * RUN * ((place // RUN) % 2)
     y, z = (place // RUN) % RING_Y, (place // (RING_Y * RUN)) * RUN + place % RUN
@@ -270,7 +270,7 @@
     def span_of(slot):
         return pl.ds(pl.multiple_of(slot * TOK, TOK), TOK)
 
-    slot, count = 0, jnp.int32(0)
+    slot, count, raw = 0, jnp.int32(0), []
     for block, amount in zip(blocks, plan["counts"]):
         for part in range(amount):
             dz, other = plan["offsets"][slot]
@@ -279,9 +279,7 @@
             numbers[slot] = number
             key = block[part * TOK : (part + 1) * TOK, :HD]
             value = jnp.concatenate([block[part * TOK : (part + 1) * TOK, HD:], ones], axis=1)
-            if carrier is not None:
-                raw_keys[slot * TOK : (slot + 1) * TOK, :] = key
-                raw_values[slot * TOK : (slot + 1) * TOK, :] = value
+            raw.append((key, value))
             keys[span_of(count), :] = key
             values[span_of(count), :] = value
             count = count + (number < bound).astype(jnp.int32)
@@ -292,30 +290,28 @@
             values[span_of(count + more), :] = jnp.zeros((TOK, 2 * HD), jnp.bfloat16)
 
     if rows_too:
-        decode_query = jnp.concatenate(head_rows(own_pack) + head_rows(mate_pack), axis=0)
+        decode_query[...] = jnp.concatenate(head_rows(own_pack) + head_rows(mate_pack), axis=0)
     if carrier is not None:
         own_reach, mate_reach = reach_of(own_pack), reach_of(mate_pack)
         lane = lax.broadcasted_iota(jnp.int32, (ROW, TOK), 1).astype(jnp.float32)
 
-    def decode():
+    def decode(side):
+        reach = jnp.where(side == 0, own_reach, mate_reach)
         allowed = []
         for slot in range(len(plan["offsets"])):
-            base = (numbers[slot] * TOK).astype(jnp.float32)
-            fits = []
-            for reach in (own_reach, mate_reach):
-                left = reach - base
-                fits += [lane < jnp.concatenate([left, left], axis=1)] * GROUP
-            allowed.append(jnp.concatenate(fits, axis=0))
-        spans = [slice(i * TOK, (i + 1) * TOK) for i in range(len(plan["offsets"]))]
+            left = reach - (numbers[slot] * TOK).astype(jnp.float32)
+            fits = lane < jnp.concatenate([left, left], axis=1)
+            allowed.append(jnp.concatenate([fits] * GROUP, axis=0))
+        rows = pl.ds(pl.multiple_of(side * GROUP * ROW, GROUP * ROW), GROUP * ROW)
         attend(
-            decode_query,
-            [raw_keys[span, :] for span in spans],
-            [raw_values[span, :] for span in spans],
+            decode_query[rows, :],
+            [key for key, _ in raw],
+            [value for _, value in raw],
             allowed,
             True,
             rows_top,
             rows_mixed,
-            slice(0, 2 * GROUP * ROW),
+            rows,
         )
 
     def prefill(pack, some_keys, some_values, allowed, top_ref, mixed_ref, at_once, active=None):
@@ -334,6 +330,9 @@
                     pl.ds(pl.multiple_of(head * TOK, TOK), TOK),
                     active,
                 )
+            if carrier is not None:
+                for number in range(2 * at_once // GROUP):
+                    decode(turn * 2 * at_once // GROUP + number)
             return carry
 
         if at_once == GROUP:
@@ -366,7 +365,6 @@
             lax.fori_loop(0, (count + size - 1) // size, turn, 0)
         else:
             turn(0, 0, count > 0)
-            decode()
 
     if extra:
         nodes = per_row(node_ref, place * ROW)
@@ -384,7 +382,7 @@
         extra_keys = jnp.concatenate([rim[:, :HD], row_pairs[:, :HD], pad], axis=0)
         extra_values = jnp.concatenate([rim[:, HD:], row_pairs[:, HD:], pad], axis=0)
         attend(
-            decode_query[: GROUP * ROW],
+            decode_query[: GROUP * ROW, :],
             [extra_keys],
             [jnp.concatenate([extra_values, extra_ones], axis=1)],
             [jnp.concatenate([same] * GROUP, axis=0)],
@@ -457,8 +455,7 @@
         scratch_shapes=[
             pltpu.VMEM(((total + size) * TOK, HD), jnp.bfloat16),
             pltpu.VMEM(((total + size) * TOK, 2 * HD), jnp.bfloat16),
-            pltpu.VMEM((total * TOK, HD), jnp.bfloat16),
-            pltpu.VMEM((total * TOK, 2 * HD), jnp.bfloat16),
+            pltpu.VMEM((2 * GROUP * ROW, HD), jnp.bfloat16),
             pltpu.SMEM((16,), jnp.int32),
         ],
         input_output_aliases=aliases,
@@ -594,7 +591,7 @@
     late, late_steps = [above_three, below_three, end], [(-3, 0), (3, 0), (4, 0)]
     state = run(late, late_steps, state, mate=True, carrier="mate", size=3)
     last, last_steps = [third, fourth], [(-3, 1), (3, 1), (4, 1)]
-    state, packed = run(last, last_steps, state, mate=True, carrier="mate", finish=True, size=3)
+    state, packed = run(last, last_steps, state, mate=True, carrier="mate", finish=True, size=3, at_once=GROUP)
     sent = swap(packed, RUN)
     packed, state = lax.optimization_barrier((packed, state))
     state = run(

time: 98 us -> 96.5 us (0.985)
  Pallas kernels: 41.6 us -> 39.4 us
    pallas_call x6, Pallas kernels: 33.3 us -> 31.2 us  [stage(): pl.pallas_call(functools.partial(stage_kernel, plan), in_specs=[IN_SMEM]...]
  transfers between devices with their start and end apart: 23 -> 23, of which waited for: 9 -> 9; matrix products, arithmetic and copies ran while one was open for 4% -> 4% of each run, Pallas kernels for 37% -> 36%
where the time goes in v1:
time: 96.5 us; the launch traced here: 96.2 us
  Pallas kernels  39.4 us (41%)
  starting transfers between devices  29.1 us (30%)
  waiting for transfers between devices  20.1 us (21%)
  local copies, waits for them, and re-layouts  5.87 us (6%)
    pallas_call x6, Pallas kernels, stage(): pl.pallas_call(functools.partial(stage_kernel, plan), in_specs=[IN_SMEM]...  31.2 us
    ppermute x4, waiting for transfers between devices, move_x(): lax.ppermute(block, 'tp', [(i, (i + 2 * step) % 8) for i in range(8)])  12.4 us
    ppermute x8, starting transfers between devices, move(): return lax.ppermute(block, PLACE, route)  11.3 us
    ppermute x6, starting transfers between devices, swap(): return lax.ppermute(block, PLACE, [(i, i ^ bits) for i in range(32)])  8.87 us
    pallas_call x4, Pallas kernels, project(): pl.pallas_call(functools.partial(project_kernel, spans, shifts, later, he...  6.85 us
    ppermute x4, starting transfers between devices, move_x(): lax.ppermute(block, 'tp', [(i, (i + 2 * step) % 8) for i in range(8)])  4.94 us
    unnamed x18, local copies, waits for them, and re-layouts  4.86 us
    ppermute x8, waiting for transfers between devices, move(): return lax.ppermute(block, PLACE, route)  4.3 us
  transfers between devices with their start and end apart: 23, of which 9 were waited for; matrix products, arithmetic and copies ran while one was open for 4% of the time, Pallas kernels for 36%

profile of v1, /device:TPU:240, one launch (start us, length us, event | category | flops | bytes accessed | tf_op | source)
XLA Modules:
  0.0 96.2 jit_solution(5355567250285788452)
XLA Ops:
  0.6 1.1 %constant_dynamic-update-slice_fusion.1 = bf16[272,1024]{1,0:T(8,128)(2,1)S(1)} fusion(bf16[256,1024]{1,0:T(8,128)(2,1)} %refs_0_.2), kind=kLoop, calls=%fused_computation.9 | loop fusion | bytes 1048576
  1.7 0.8 constant_dynamic-update-slice_fusion
  2.5 0.0 collective-permute-start.2
  2.5 2.8 %collective-permute-start.1 = (bf16[272,1024]{1,0:T(8,128)(2,1)S(1)}, bf16[272,1024]{1,0:T(8,128)(2,1)S(1)}, u32[]{:S(2)}, u32[]{:S(2)}) collective-permute-start(bf16[272,1024]{1,0:T(8,128)(2,1)S(1)} %constant_dynamic-update-slice_fusion), channel_id=1, source_target_pairs={{0,6},{1,7},{2,0},{3,1},{4,2},{5,3},{6,4},{7,5},{8,14},{9,15},{10,... | collective-permute-start | bytes 1671176 | tf_op jit(solution)/shard_map/ppermute | solution.py:49
  5.2 0.0 collective-permute-start
  5.3 0.7 convert_bitcast_fusion
  5.9 0.1 copy.27
  6.0 0.1 broadcast_in_dim.3
  6.2 0.0 copy-start.4
  6.2 0.0 copy-start.5
  6.2 2.8 %copy.32 = bf16[1024,8,2,128]{3,1,2,0:T(8,128)(2,1)S(1)} copy(bf16[1024,8,2,128]{3,2,1,0:T(2,128)(2,1)} %bitcast.18) | data formatting | bytes 8388608
  9.0 0.0 copy-start
  9.0 0.0 copy-start.1
  9.1 0.0 collective-permute-done.2.refs_2_
  9.1 0.9 copy-done
  10.0 2.0 %shard_map.104 = (f32[272,256]{1,0:T(8,128)S(1)}, f32[272,128]{1,0:T(8,128)S(1)}) custom-call(s32[1]{0:T(128)} %bitcast.1.tp_ref, bf16[256,1024]{1,0:T(8,128)(2,1)S(1)} %copy-done, bf16[16,1024]{1,0:T(8,128)(2,1)S(1)} %copy-done.1, bf16[272,1024]{1,0:T(8,128)(2,1)S(1)} %collective-permute-done.2.refs_2_, bf16[8192,256]{1,0:T(8,128)(2,1)S(1)} %bitcast.15, ...), custom_call_target="tpu_custom_call" | custom-call | flops 285212672 | bytes 2200000 | tf_op jit(solution)/shard_map/pallas_call | solution.py:152
  12.0 5.8 %collective-permute-done.1.refs_1_ = bf16[272,1024]{1,0:T(8,128)(2,1)S(1)} collective-permute-done((bf16[272,1024]{1,0:T(8,128)(2,1)S(1)}, bf16[272,1024]{1,0:T(8,128)(2,1)S(1)}, u32[]{:S(2)}, u32[]{:S(2)}) %collective-permute-start.1) | collective-permute-done | bytes 557088 | tf_op jit(solution)/shard_map/ppermute | solution.py:49
  17.8 3.4 %collective-permute-done.refs_0_ = bf16[272,1024]{1,0:T(8,128)(2,1)S(1)} collective-permute-done((bf16[272,1024]{1,0:T(8,128)(2,1)S(1)}, bf16[272,1024]{1,0:T(8,128)(2,1)S(1)}, u32[]{:S(2)}, u32[]{:S(2)}) %collective-permute-start) | collective-permute-done | bytes 557088 | tf_op jit(solution)/shard_map/ppermute | solution.py:49
  21.2 0.0 collective-permute-start.5
  21.2 0.5 collective-permute-start.6
  21.8 0.4 collective-permute-start.4
  22.1 1.8 %collective-permute-start.3 = (bf16[128,1024]{1,0:T(8,128)(2,1)S(1)}, bf16[128,1024]{1,0:T(8,128)(2,1)S(1)}, u32[]{:S(2)}, u32[]{:S(2)}) collective-permute-start(bf16[128,1024]{1,0:T(8,128)(2,1)S(1)} %slice.12), channel_id=1, source_target_pairs={{0,2},{1,3},{2,4},{3,5},{4,6},{5,7},{6,0},{7,1},{8,10},{9,11},{10,... | collective-permute-start | bytes 786440 | tf_op jit(solution)/shard_map/ppermute | solution.py:49
  24.0 0.0 collective-permute-done.5.refs_2_
  24.0 0.0 collective-permute-done.6.refs_3_
  24.0 4.2 %shard_map.105 = (f32[272,256]{1,0:T(8,128)S(1)}, f32[272,128]{1,0:T(8,128)S(1)}, bf16[2,1024,256]{2,1,0:T(8,128)(2,1)S(1)}) custom-call(s32[1]{0:T(128)} %bitcast.1.tp_ref, bf16[272,1024]{1,0:T(8,128)(2,1)S(1)} %collective-permute-done.refs_0_, bf16[272,1024]{1,0:T(8,128)(2,1)S(1)} %collective-permute-done.1.refs_1_, ...), custom_call_target="tpu_custom_call" | custom-call | flops 570425344 | bytes 4400000 | tf_op jit(solution)/shard_map/pallas_call | solution.py:152
  28.1 3.2 %collective-permute-done.3.refs_0_ = bf16[128,1024]{1,0:T(8,128)(2,1)S(1)} collective-permute-done((bf16[128,1024]{1,0:T(8,128)(2,1)S(1)}, bf16[128,1024]{1,0:T(8,128)(2,1)S(1)}, u32[]{:S(2)}, u32[]{:S(2)}) %collective-permute-start.3) | collective-permute-done | bytes 262176 | tf_op jit(solution)/shard_map/ppermute | solution.py:49
  31.4 0.0 collective-permute-done.4.refs_1_
  31.4 0.0 copy-start.2
  31.4 0.1 collective-permute-start.7
  31.5 1.4 %collective-permute-start.13 = (bf16[288,1024]{1,0:T(8,128)(2,1)S(1)}, bf16[288,1024]{1,0:T(8,128)(2,1)S(1)}, u32[]{:S(2)}, u32[]{:S(2)}) collective-permute-start(bf16[288,1024]{1,0:T(8,128)(2,1)S(1)} %fusion.1.refs_1_.refs_5_.refs_2_.refs_3_.refs_12_), channel_id=1, source_target_pairs={{0,32},{8,40},{16,48},{24,56},{32,0},{40,8},{48,16},{56,24},{64,96... | collective-permute-start | bytes 1769480 | tf_op jit(solution)/shard_map/ppermute | solution.py:534
  32.9 0.3 shard_map.106
  33.3 0.2 collective-permute-done.7.refs_0_
  33.5 0.3 shard_map.107
  33.8 1.1 %collective-permute-start.9 = (bf16[256,256]{1,0:T(8,128)(2,1)S(1)}, bf16[256,256]{1,0:T(8,128)(2,1)S(1)}, u32[]{:S(2)}, u32[]{:S(2)}) collective-permute-start(bf16[256,256]{1,0:T(8,128)(2,1)S(1)} %get-tuple-element.86.refs_0_), channel_id=1, source_target_pairs={{0,152},{8,0},{16,8},{24,16},{128,24},{136,128},{144,136},{152,144... | collective-permute-start | bytes 393224 | tf_op jit(solution)/shard_map/ppermute | solution.py:45
  34.9 2.2 %collective-permute-start.8 = (bf16[256,256]{1,0:T(8,128)(2,1)S(1)}, bf16[256,256]{1,0:T(8,128)(2,1)S(1)}, u32[]{:S(2)}, u32[]{:S(2)}) collective-permute-start(bf16[256,256]{1,0:T(8,128)(2,1)S(1)} %get-tuple-element.86.refs_0_), channel_id=1, source_target_pairs={{0,8},{8,16},{16,24},{24,128},{128,136},{136,144},{144,152},{152,0... | collective-permute-start | bytes 393224 | tf_op jit(solution)/shard_map/ppermute | solution.py:45
  37.1 3.3 %collective-permute-start.10 = (bf16[16,256]{1,0:T(8,128)(2,1)S(1)}, bf16[16,256]{1,0:T(8,128)(2,1)S(1)}, u32[]{:S(2)}, u32[]{:S(2)}) collective-permute-start(bf16[16,256]{1,0:T(8,128)(2,1)S(1)} %get-tuple-element.90.refs_15_), channel_id=1, source_target_pairs={{0,8},{8,16},{16,24},{24,32},{32,40},{40,48},{48,56},{56,64},{64,7... | collective-permute-start | bytes 24584 | tf_op jit(solution)/shard_map/ppermute | solution.py:571
  40.5 1.6 %shard_map.108 = (f32[2048,128]{1,0:T(8,128)S(1)}, f32[2048,256]{1,0:T(8,128)S(1)}) custom-call(s32[1]{0:T(128)} %bitcast.place_ref, bf16[256,256]{1,0:T(8,128)(2,1)S(1)} %get-tuple-element.86.refs_0_, bf16[288,1024]{1,0:T(8,128)(2,1)S(1)} %fusion.1.refs_1_.refs_5_.refs_2_.refs_3_.refs_12_), custom_call_target="tpu_custom_call" | custom-call | flops 536870912 | bytes 2000000 | tf_op jit(solution)/shard_map/pallas_call | solution.py:450
  42.0 0.7 collective-permute-done.10.refs_14_
  42.7 0.0 collective-permute-done.9.refs_2_
  42.7 2.7 %collective-permute-start.11 = (bf16[256,256]{1,0:T(8,128)(2,1)S(1)}, bf16[256,256]{1,0:T(8,128)(2,1)S(1)}, u32[]{:S(2)}, u32[]{:S(2)}) collective-permute-start(bf16[256,256]{1,0:T(8,128)(2,1)S(1)} %collective-permute-done.8.refs_1_), channel_id=1, source_target_pairs={{0,8},{8,16},{16,24},{24,128},{128,136},{136,144},{144,152},{152,0... | collective-permute-start | bytes 393224 | tf_op jit(solution)/shard_map/ppermute | solution.py:45
  45.4 0.0 collective-permute-start.12
  45.4 0.6 collective-permute-start.14
  46.1 1.2 %collective-permute-done.13.refs_6_.refs_3_.refs_4_.refs_13_ = bf16[288,1024]{1,0:T(8,128)(2,1)S(1)} collective-permute-done((bf16[288,1024]{1,0:T(8,128)(2,1)S(1)}, bf16[288,1024]{1,0:T(8,128)(2,1)S(1)}, u32[]{:S(2)}, u32[]{:S(2)}) %collective-permute-start.13) | collective-permute-done | bytes 589856 | tf_op jit(solution)/shard_map/ppermute | solution.py:534
  47.3 0.6 collective-permute-done.11.refs_3_
  47.9 3.7 %collective-permute-done.12.refs_4_ = bf16[256,256]{1,0:T(8,128)(2,1)S(1)} collective-permute-done((bf16[256,256]{1,0:T(8,128)(2,1)S(1)}, bf16[256,256]{1,0:T(8,128)(2,1)S(1)}, u32[]{:S(2)}, u32[]{:S(2)}) %collective-permute-start.12) | collective-permute-done | bytes 131104 | tf_op jit(solution)/shard_map/ppermute | solution.py:45
  51.6 0.0 collective-permute-start.16
  51.6 2.0 %collective-permute-start.17 = (bf16[256,256]{1,0:T(8,128)(2,1)S(1)}, bf16[256,256]{1,0:T(8,128)(2,1)S(1)}, u32[]{:S(2)}, u32[]{:S(2)}) collective-permute-start(bf16[256,256]{1,0:T(8,128)(2,1)S(1)} %collective-permute-done.12.refs_4_), channel_id=1, source_target_pairs={{0,152},{8,0},{16,8},{24,16},{128,24},{136,128},{144,136},{152,144... | collective-permute-start | bytes 393224 | tf_op jit(solution)/shard_map/ppermute | solution.py:45
  53.6 0.6 collective-permute-start.15
  54.3 4.9 %shard_map.109 = (f32[2048,128]{1,0:T(8,128)S(1)}, f32[2048,256]{1,0:T(8,128)S(1)}, f32[256,128]{1,0:T(8,128)S(1)}, f32[256,256]{1,0:T(8,128)S(1)}) custom-call(s32[1]{0:T(128)} %bitcast.place_ref, bf16[256,256]{1,0:T(8,128)(2,1)S(1)} %get-tuple-element.86.refs_0_, bf16[256,256]{1,0:T(8,128)(2,1)S(1)} %collective-permute-done.8.refs_1_, ...), custom_call_target="tpu_custom_call" | custom-call | flops 2684354560 | bytes 2000000 | tf_op jit(solution)/shard_map/pallas_call | solution.py:450
  59.1 0.0 collective-permute-done.17.refs_1_.refs_8_
  59.2 0.1 collective-permute-start.19
  59.3 3.2 %collective-permute-start.18 = (bf16[128,256]{1,0:T(8,128)(2,1)S(1)}, bf16[128,256]{1,0:T(8,128)(2,1)S(1)}, u32[]{:S(2)}, u32[]{:S(2)}) collective-permute-start(bf16[128,256]{1,0:T(8,128)(2,1)S(1)} %slice.14), channel_id=1, source_target_pairs={{0,8},{8,16},{16,24},{24,128},{128,136},{136,144},{144,152},{152,0... | collective-permute-start | bytes 196616 | tf_op jit(solution)/shard_map/ppermute | solution.py:45
  62.5 1.8 %collective-permute-start.20 = (bf16[512,256]{1,0:T(8,128)(2,1)S(1)}, bf16[512,256]{1,0:T(8,128)(2,1)S(1)}, u32[]{:S(2)}, u32[]{:S(2)}) collective-permute-start(bf16[512,256]{1,0:T(8,128)(2,1)S(1)} %pad_maximum_fusion.3), channel_id=1, source_target_pairs={{0,96},{8,104},{16,112},{24,120},{32,64},{40,72},{48,80},{56,88},{... | collective-permute-start | bytes 786440 | tf_op jit(solution)/shard_map/ppermute | solution.py:534
  64.3 0.0 collective-permute-done.15.refs_1_.refs_6_
  64.3 0.0 collective-permute-done.14.refs_0_.refs_5_
  64.3 4.5 %shard_map.110 = (f32[2048,128]{1,0:T(8,128)S(1)}, f32[2048,256]{1,0:T(8,128)S(1)}, f32[256,128]{1,0:T(8,128)S(1)}, f32[256,256]{1,0:T(8,128)S(1)}) custom-call(s32[1]{0:T(128)} %bitcast.place_ref, bf16[768,256]{1,0:T(8,128)(2,1)S(1)} %collective-permute-done.14.refs_0_.refs_5_, ...), custom_call_target="tpu_custom_call", output_to_operand_aliasing={{0}: (5, {}), {1}: (6, {}), {2}: (7, {}), {3}: (8, {})} | custom-call | flops 2684354560 | bytes 2000000 | tf_op jit(solution)/shard_map/pallas_call | solution.py:450
  68.9 0.7 collective-permute-start.21
  69.5 3.1 %shard_map.111 = (f32[2048,128]{1,0:T(8,128)S(1)}, f32[2048,256]{1,0:T(8,128)S(1)}, f32[256,128]{1,0:T(8,128)S(1)}, f32[256,256]{1,0:T(8,128)S(1)}) custom-call(s32[1]{0:T(128)} %bitcast.place_ref, bf16[256,256]{1,0:T(8,128)(2,1)S(1)} %collective-permute-done.16.refs_0_.refs_7_, ...), custom_call_target="tpu_custom_call", output_to_operand_aliasing={{0}: (6, {}), {1}: (7, {}), {2}: (8, {}), {3}: (9, {})} | custom-call | flops 1610612736 | bytes 2000000 | tf_op jit(solution)/shard_map/pallas_call | solution.py:450
  72.6 1.3 %collective-permute-done.21.refs_1_.refs_11_ = bf16[256,256]{1,0:T(8,128)(2,1)S(1)} collective-permute-done((bf16[256,256]{1,0:T(8,128)(2,1)S(1)}, bf16[256,256]{1,0:T(8,128)(2,1)S(1)}, u32[]{:S(2)}, u32[]{:S(2)}) %collective-permute-start.21) | collective-permute-done | bytes 131104 | tf_op jit(solution)/shard_map/ppermute | solution.py:534
  73.9 0.0 collective-permute-done.20.refs_0_.refs_10_
  73.9 3.5 %shard_map.112 = (bf16[2272,128]{1,0:T(8,128)(2,1)S(1)}, f32[2048,128]{1,0:T(8,128)S(1)}, f32[2048,256]{1,0:T(8,128)S(1)}, f32[256,128]{1,0:T(8,128)S(1)}, f32[256,256]{1,0:T(8,128)S(1)}) custom-call(s32[1]{0:T(128)} %bitcast.place_ref, ...), custom_call_target="tpu_custom_call", output_to_operand_aliasing={{1}: (5, {}), {2}: (6, {}), {3}: (7, {}), {4}: (8, {})} | custom-call | flops 1610612736 | bytes 2000000 | tf_op jit(solution)/shard_map/pallas_call | solution.py:450
  77.4 3.8 %collective-permute-start.22 = (bf16[2272,128]{1,0:T(8,128)(2,1)S(1)}, bf16[2272,128]{1,0:T(8,128)(2,1)S(1)}, u32[]{:S(2)}, u32[]{:S(2)}) collective-permute-start(bf16[2272,128]{1,0:T(8,128)(2,1)S(1)} %get-tuple-element.125), channel_id=1, source_target_pairs={{0,32},{8,40},{16,48},{24,56},{32,0},{40,8},{48,16},{56,24},{64,96... | collective-permute-start | bytes 1744904 | tf_op jit(solution)/shard_map/ppermute | solution.py:534
  81.2 13.6 %shard_map.113 = (f32[2048,128]{1,0:T(8,128)S(1)}, f32[2048,256]{1,0:T(8,128)S(1)}, f32[256,128]{1,0:T(8,128)S(1)}, f32[256,256]{1,0:T(8,128)S(1)}) custom-call(s32[1]{0:T(128)} %bitcast.place_ref, s32[512]{0:T(512)S(1)} %copy-done.3, ...), custom_call_target="tpu_custom_call", output_to_operand_aliasing={{0}: (17, {}), {1}: (18, {}), {2}: (19, {}), {3}: (20, {})} | custom-call | flops 8053063680 | bytes 2000000 | tf_op jit(solution)/shard_map/pallas_call | solution.py:450
  94.8 1.4 %shard_map.114 = (bf16[256,1024]{1,0:T(8,128)(2,1)}, bf16[16,1024]{1,0:T(8,128)(2,1)}) custom-call(f32[2048,128]{1,0:T(8,128)S(1)} %get-tuple-element.134.own_top, f32[2048,256]{1,0:T(8,128)S(1)} %get-tuple-element.135.own_mixed, f32[256,128]{1,0:T(8,128)S(1)} %get-tuple-element.136.rows_top, f32[256,256]{1,0:T(8,128)S(1)} %get-tuple-element.137.rows_mixed, ...), custom_call_target="tpu_custom_call" | custom-call | tf_op jit(solution)/shard_map/pallas_call | solution.py:504
  (27 shorter events, 0.3 us)
Async XLA Ops:
  0.6 5.5 %copy-start.6 = (f32[8192]{0:T(1024)S(1)}, f32[8192]{0:T(1024)}, u32[]{:S(2)}) copy-start(f32[8192]{0:T(1024)} %param.11) | copy-start | bytes 98308
  2.5 6.6 %collective-permute-start.2 = (bf16[272,1024]{1,0:T(8,128)(2,1)S(1)}, bf16[272,1024]{1,0:T(8,128)(2,1)S(1)}, u32[]{:S(2)}, u32[]{:S(2)}) collective-permute-start(bf16[272,1024]{1,0:T(8,128)(2,1)S(1)} %constant_dynamic-update-slice_fusion), channel_id=1, source_target_pairs={{0,1},{1,0},{2,3},{3,2},{4,5},{5,4},{6,7},{7,6},{8,9},{9,8},{10,11... | collective-permute-start | bytes 1671176 | tf_op jit(solution)/shard_map/ppermute | solution.py:53
  2.5 15.3 %collective-permute-start.1 = (bf16[272,1024]{1,0:T(8,128)(2,1)S(1)}, bf16[272,1024]{1,0:T(8,128)(2,1)S(1)}, u32[]{:S(2)}, u32[]{:S(2)}) collective-permute-start(bf16[272,1024]{1,0:T(8,128)(2,1)S(1)} %constant_dynamic-update-slice_fusion), channel_id=1, source_target_pairs={{0,6},{1,7},{2,0},{3,1},{4,2},{5,3},{6,4},{7,5},{8,14},{9,15},{10,... | collective-permute-start | bytes 1671176 | tf_op jit(solution)/shard_map/ppermute | solution.py:49
  5.2 16.0 %collective-permute-start = (bf16[272,1024]{1,0:T(8,128)(2,1)S(1)}, bf16[272,1024]{1,0:T(8,128)(2,1)S(1)}, u32[]{:S(2)}, u32[]{:S(2)}) collective-permute-start(bf16[272,1024]{1,0:T(8,128)(2,1)S(1)} %constant_dynamic-update-slice_fusion), channel_id=1, source_target_pairs={{0,2},{1,3},{2,4},{3,5},{4,6},{5,7},{6,0},{7,1},{8,10},{9,11},{10,... | collective-permute-start | bytes 1671176 | tf_op jit(solution)/shard_map/ppermute | solution.py:49
  6.2 2.8 %copy-start.4 = (bf16[256,1024]{1,0:T(8,128)(2,1)S(1)}, bf16[256,1024]{1,0:T(8,128)(2,1)}, u32[]{:S(2)}) copy-start(bf16[256,1024]{1,0:T(8,128)(2,1)} %param.14) | copy-start | bytes 1572868
  6.2 2.8 %copy-start.5 = (bf16[16,1024]{1,0:T(8,128)(2,1)S(1)}, bf16[16,1024]{1,0:T(8,128)(2,1)}, u32[]{:S(2)}) copy-start(bf16[16,1024]{1,0:T(8,128)(2,1)} %param.15) | copy-start | bytes 98308
  9.0 1.0 %copy-start = (bf16[256,1024]{1,0:T(8,128)(2,1)S(1)}, bf16[256,1024]{1,0:T(8,128)(2,1)}, u32[]{:S(2)}) copy-start(bf16[256,1024]{1,0:T(8,128)(2,1)} %refs_0_.2) | copy-start | bytes 1572868
  9.0 1.0 %copy-start.1 = (bf16[16,1024]{1,0:T(8,128)(2,1)S(1)}, bf16[16,1024]{1,0:T(8,128)(2,1)}, u32[]{:S(2)}) copy-start(bf16[16,1024]{1,0:T(8,128)(2,1)} %refs_1_.1) | copy-start | bytes 98308
  21.2 2.7 %collective-permute-start.5 = (bf16[272,1024]{1,0:T(8,128)(2,1)S(1)}, bf16[272,1024]{1,0:T(8,128)(2,1)S(1)}, u32[]{:S(2)}, u32[]{:S(2)}) collective-permute-start(bf16[272,1024]{1,0:T(8,128)(2,1)S(1)} %collective-permute-done.refs_0_), channel_id=1, source_target_pairs={{0,1},{1,0},{2,3},{3,2},{4,5},{5,4},{6,7},{7,6},{8,9},{9,8},{10,11... | collective-permute-start | bytes 1671176 | tf_op jit(solution)/shard_map/ppermute | solution.py:53
  21.2 2.8 %collective-permute-start.6 = (bf16[272,1024]{1,0:T(8,128)(2,1)S(1)}, bf16[272,1024]{1,0:T(8,128)(2,1)S(1)}, u32[]{:S(2)}, u32[]{:S(2)}) collective-permute-start(bf16[272,1024]{1,0:T(8,128)(2,1)S(1)} %collective-permute-done.1.refs_1_), channel_id=1, source_target_pairs={{0,1},{1,0},{2,3},{3,2},{4,5},{5,4},{6,7},{7,6},{8,9},{9,8},{10,11... | collective-permute-start | bytes 1671176 | tf_op jit(solution)/shard_map/ppermute | solution.py:53
  21.8 9.6 %collective-permute-start.4 = (bf16[144,1024]{1,0:T(8,128)(2,1)S(1)}, bf16[144,1024]{1,0:T(8,128)(2,1)S(1)}, u32[]{:S(2)}, u32[]{:S(2)}) collective-permute-start(bf16[144,1024]{1,0:T(8,128)(2,1)S(1)} %slice.13), channel_id=1, source_target_pairs={{0,6},{1,7},{2,0},{3,1},{4,2},{5,3},{6,4},{7,5},{8,14},{9,15},{10,... | collective-permute-start | bytes 884744 | tf_op jit(solution)/shard_map/ppermute | solution.py:49
  22.1 9.2 %collective-permute-start.3 = (bf16[128,1024]{1,0:T(8,128)(2,1)S(1)}, bf16[128,1024]{1,0:T(8,128)(2,1)S(1)}, u32[]{:S(2)}, u32[]{:S(2)}) collective-permute-start(bf16[128,1024]{1,0:T(8,128)(2,1)S(1)} %slice.12), channel_id=1, source_target_pairs={{0,2},{1,3},{2,4},{3,5},{4,6},{5,7},{6,0},{7,1},{8,10},{9,11},{10,... | collective-permute-start | bytes 786440 | tf_op jit(solution)/shard_map/ppermute | solution.py:49
  31.4 2.1 %copy-start.2 = (f32[128]{0:T(128)S(1)}, f32[128]{0:T(128)}, u32[]{:S(2)}) copy-start(f32[128]{0:T(128)} %param.13) | copy-start | bytes 1540
  31.4 2.0 %collective-permute-start.7 = (bf16[272,1024]{1,0:T(8,128)(2,1)S(1)}, bf16[272,1024]{1,0:T(8,128)(2,1)S(1)}, u32[]{:S(2)}, u32[]{:S(2)}) collective-permute-start(bf16[272,1024]{1,0:T(8,128)(2,1)S(1)} %pad_maximum_fusion), channel_id=1, source_target_pairs={{0,1},{1,0},{2,3},{3,2},{4,5},{5,4},{6,7},{7,6},{8,9},{9,8},{10,11... | collective-permute-start | bytes 1671176 | tf_op jit(solution)/shard_map/ppermute | solution.py:53
  31.5 15.7 %collective-permute-start.13 = (bf16[288,1024]{1,0:T(8,128)(2,1)S(1)}, bf16[288,1024]{1,0:T(8,128)(2,1)S(1)}, u32[]{:S(2)}, u32[]{:S(2)}) collective-permute-start(bf16[288,1024]{1,0:T(8,128)(2,1)S(1)} %fusion.1.refs_1_.refs_5_.refs_2_.refs_3_.refs_12_), channel_id=1, source_target_pairs={{0,32},{8,40},{16,48},{24,56},{32,0},{40,8},{48,16},{56,24},{64,96... | collective-permute-start | bytes 1769480 | tf_op jit(solution)/shard_map/ppermute | solution.py:534
  33.8 8.8 %collective-permute-start.9 = (bf16[256,256]{1,0:T(8,128)(2,1)S(1)}, bf16[256,256]{1,0:T(8,128)(2,1)S(1)}, u32[]{:S(2)}, u32[]{:S(2)}) collective-permute-start(bf16[256,256]{1,0:T(8,128)(2,1)S(1)} %get-tuple-element.86.refs_0_), channel_id=1, source_target_pairs={{0,152},{8,0},{16,8},{24,16},{128,24},{136,128},{144,136},{152,144... | collective-permute-start | bytes 393224 | tf_op jit(solution)/shard_map/ppermute | solution.py:45
  34.9 7.8 %collective-permute-start.8 = (bf16[256,256]{1,0:T(8,128)(2,1)S(1)}, bf16[256,256]{1,0:T(8,128)(2,1)S(1)}, u32[]{:S(2)}, u32[]{:S(2)}) collective-permute-start(bf16[256,256]{1,0:T(8,128)(2,1)S(1)} %get-tuple-element.86.refs_0_), channel_id=1, source_target_pairs={{0,8},{8,16},{16,24},{24,128},{128,136},{136,144},{144,152},{152,0... | collective-permute-start | bytes 393224 | tf_op jit(solution)/shard_map/ppermute | solution.py:45
  37.1 5.5 %collective-permute-start.10 = (bf16[16,256]{1,0:T(8,128)(2,1)S(1)}, bf16[16,256]{1,0:T(8,128)(2,1)S(1)}, u32[]{:S(2)}, u32[]{:S(2)}) collective-permute-start(bf16[16,256]{1,0:T(8,128)(2,1)S(1)} %get-tuple-element.90.refs_15_), channel_id=1, source_target_pairs={{0,8},{8,16},{16,24},{24,32},{32,40},{40,48},{48,56},{56,64},{64,7... | collective-permute-start | bytes 24584 | tf_op jit(solution)/shard_map/ppermute | solution.py:571
  42.7 5.2 %collective-permute-start.11 = (bf16[256,256]{1,0:T(8,128)(2,1)S(1)}, bf16[256,256]{1,0:T(8,128)(2,1)S(1)}, u32[]{:S(2)}, u32[]{:S(2)}) collective-permute-start(bf16[256,256]{1,0:T(8,128)(2,1)S(1)} %collective-permute-done.8.refs_1_), channel_id=1, source_target_pairs={{0,8},{8,16},{16,24},{24,128},{128,136},{136,144},{144,152},{152,0... | collective-permute-start | bytes 393224 | tf_op jit(solution)/shard_map/ppermute | solution.py:45
  45.4 6.2 %collective-permute-start.12 = (bf16[256,256]{1,0:T(8,128)(2,1)S(1)}, bf16[256,256]{1,0:T(8,128)(2,1)S(1)}, u32[]{:S(2)}, u32[]{:S(2)}) collective-permute-start(bf16[256,256]{1,0:T(8,128)(2,1)S(1)} %collective-permute-done.9.refs_2_), channel_id=1, source_target_pairs={{0,152},{8,0},{16,8},{24,16},{128,24},{136,128},{144,136},{152,144... | collective-permute-start | bytes 393224 | tf_op jit(solution)/shard_map/ppermute | solution.py:45
  45.4 18.9 %collective-permute-start.14 = (bf16[768,256]{1,0:T(8,128)(2,1)S(1)}, bf16[768,256]{1,0:T(8,128)(2,1)S(1)}, u32[]{:S(2)}, u32[]{:S(2)}) collective-permute-start(bf16[768,256]{1,0:T(8,128)(2,1)S(1)} %pad_maximum_fusion.1), channel_id=1, source_target_pairs={{0,96},{8,104},{16,112},{24,120},{32,64},{40,72},{48,80},{56,88},{... | collective-permute-start | bytes 1179656 | tf_op jit(solution)/shard_map/ppermute | solution.py:534
  51.6 7.6 %collective-permute-start.16 = (bf16[256,256]{1,0:T(8,128)(2,1)S(1)}, bf16[256,256]{1,0:T(8,128)(2,1)S(1)}, u32[]{:S(2)}, u32[]{:S(2)}) collective-permute-start(bf16[256,256]{1,0:T(8,128)(2,1)S(1)} %collective-permute-done.11.refs_3_), channel_id=1, source_target_pairs={{0,8},{8,16},{16,24},{24,128},{128,136},{136,144},{144,152},{152,0... | collective-permute-start | bytes 393224 | tf_op jit(solution)/shard_map/ppermute | solution.py:45
  51.6 7.6 %collective-permute-start.17 = (bf16[256,256]{1,0:T(8,128)(2,1)S(1)}, bf16[256,256]{1,0:T(8,128)(2,1)S(1)}, u32[]{:S(2)}, u32[]{:S(2)}) collective-permute-start(bf16[256,256]{1,0:T(8,128)(2,1)S(1)} %collective-permute-done.12.refs_4_), channel_id=1, source_target_pairs={{0,152},{8,0},{16,8},{24,16},{128,24},{136,128},{144,136},{152,144... | collective-permute-start | bytes 393224 | tf_op jit(solution)/shard_map/ppermute | solution.py:45
  53.6 10.7 %collective-permute-start.15 = (bf16[512,256]{1,0:T(8,128)(2,1)S(1)}, bf16[512,256]{1,0:T(8,128)(2,1)S(1)}, u32[]{:S(2)}, u32[]{:S(2)}) collective-permute-start(bf16[512,256]{1,0:T(8,128)(2,1)S(1)} %pad_maximum_fusion.2), channel_id=1, source_target_pairs={{0,96},{8,104},{16,112},{24,120},{32,64},{40,72},{48,80},{56,88},{... | collective-permute-start | bytes 786440 | tf_op jit(solution)/shard_map/ppermute | solution.py:534
  59.2 9.6 %collective-permute-start.19 = (bf16[128,256]{1,0:T(8,128)(2,1)S(1)}, bf16[128,256]{1,0:T(8,128)(2,1)S(1)}, u32[]{:S(2)}, u32[]{:S(2)}) collective-permute-start(bf16[128,256]{1,0:T(8,128)(2,1)S(1)} %slice.15), channel_id=1, source_target_pairs={{0,152},{8,0},{16,8},{24,16},{128,24},{136,128},{144,136},{152,144... | collective-permute-start | bytes 196616 | tf_op jit(solution)/shard_map/ppermute | solution.py:45
  59.3 9.5 %collective-permute-start.18 = (bf16[128,256]{1,0:T(8,128)(2,1)S(1)}, bf16[128,256]{1,0:T(8,128)(2,1)S(1)}, u32[]{:S(2)}, u32[]{:S(2)}) collective-permute-start(bf16[128,256]{1,0:T(8,128)(2,1)S(1)} %slice.14), channel_id=1, source_target_pairs={{0,8},{8,16},{16,24},{24,128},{128,136},{136,144},{144,152},{152,0... | collective-permute-start | bytes 196616 | tf_op jit(solution)/shard_map/ppermute | solution.py:45
  62.5 11.4 %collective-permute-start.20 = (bf16[512,256]{1,0:T(8,128)(2,1)S(1)}, bf16[512,256]{1,0:T(8,128)(2,1)S(1)}, u32[]{:S(2)}, u32[]{:S(2)}) collective-permute-start(bf16[512,256]{1,0:T(8,128)(2,1)S(1)} %pad_maximum_fusion.3), channel_id=1, source_target_pairs={{0,96},{8,104},{16,112},{24,120},{32,64},{40,72},{48,80},{56,88},{... | collective-permute-start | bytes 786440 | tf_op jit(solution)/shard_map/ppermute | solution.py:534
  68.9 5.1 %collective-permute-start.21 = (bf16[256,256]{1,0:T(8,128)(2,1)S(1)}, bf16[256,256]{1,0:T(8,128)(2,1)S(1)}, u32[]{:S(2)}, u32[]{:S(2)}) collective-permute-start(bf16[256,256]{1,0:T(8,128)(2,1)S(1)} %constant_dynamic-update-slice_fusion.2.refs_2_.refs_9_), channel_id=1, source_target_pairs={{0,96},{8,104},{16,112},{24,120},{32,64},{40,72},{48,80},{56,88},{... | collective-permute-start | bytes 393224 | tf_op jit(solution)/shard_map/ppermute | solution.py:534
  73.9 7.3 %copy-start.3 = (s32[512]{0:T(512)S(1)}, s32[512]{0:T(512)}, u32[]{:S(2)}) copy-start(s32[512]{0:T(512)} %refs_0_.3) | copy-start | bytes 6148
  77.4 17.4 %collective-permute-start.22 = (bf16[2272,128]{1,0:T(8,128)(2,1)S(1)}, bf16[2272,128]{1,0:T(8,128)(2,1)S(1)}, u32[]{:S(2)}, u32[]{:S(2)}) collective-permute-start(bf16[2272,128]{1,0:T(8,128)(2,1)S(1)} %get-tuple-element.125), channel_id=1, source_target_pairs={{0,32},{8,40},{16,48},{24,56},{32,0},{40,8},{48,16},{56,24},{64,96... | collective-permute-start | bytes 1744904 | tf_op jit(solution)/shard_map/ppermute | solution.py:534

commit v2 on v1

--- a/solution.py
+++ b/solution.py
@@ -568,11 +568,13 @@
     run = functools.partial(stage, place, (own_pack, mate_pack))
     above, below = move(pairs, 1, 0), move(pairs, -1, 0)
     state = run([pairs], [(0, 0)], None, init=True, own=True)
-    rim = lax.ppermute(row_pairs, PLACE, [(i, i + 1) for i in range(31)])
-    above, below, state, rim = lax.optimization_barrier((above, below, state, rim))
+    above, below, state, row_pairs = lax.optimization_barrier((above, below, state, row_pairs))
     above_two, below_two = move(above, 1, 0), move(below, -1, 0)
     first = swap(jnp.concatenate([pairs, above, below], axis=0), opposite)
-    above_two, below_two, mate_pack = lax.optimization_barrier((above_two, below_two, mate_pack))
+    rim = lax.ppermute(row_pairs, PLACE, [(i, i + 1) for i in range(31)])
+    above_two, below_two, mate_pack, rim = lax.optimization_barrier(
+        (above_two, below_two, mate_pack, rim)
+    )
     run = functools.partial(stage, place, (own_pack, mate_pack))
     above_three, below_three = move(above_two, 1, 0), move(below_two, -1, 0)
     second = swap(jnp.concatenate([above_two, below_two], axis=0), opposite)

time: 96.5 us -> 97.9 us (1.015)
  starting transfers between devices: 29.1 us -> 34.1 us
  waiting for transfers between devices: 20.1 us -> 16.7 us
    ppermute x8, starting transfers between devices: 11.3 us -> 14.9 us  [move(): return lax.ppermute(block, PLACE, route)]
    ppermute x6, waiting for transfers between devices: 2.49 us -> 0.59 us  [swap(): return lax.ppermute(block, PLACE, [(i, i ^ bits) for i in range(32)])]
    ppermute x1, starting transfers between devices: 3.31 us -> 4.89 us  [per_device(): rim = lax.ppermute(row_pairs, PLACE, [(i, i + 1) for i in range(31)])]
    ppermute x8, waiting for transfers between devices: 4.3 us -> 3 us  [move(): return lax.ppermute(block, PLACE, route)]
  transfers between devices with their start and end apart: 23 -> 23, of which waited for: 9 -> 8; matrix products, arithmetic and copies ran while one was open for 4% -> 4% of each run, Pallas kernels for 36% -> 35%
where the time goes in v2:
time: 97.9 us; the launch traced here: 97.6 us
  Pallas kernels  39.2 us (40%)
  starting transfers between devices  34.1 us (35%)
  waiting for transfers between devices  16.7 us (17%)
  local copies, waits for them, and re-layouts  5.87 us (6%)
    pallas_call x6, Pallas kernels, stage(): pl.pallas_call(functools.partial(stage_kernel, plan), in_specs=[IN_SMEM]...  30.9 us
    ppermute x8, starting transfers between devices, move(): return lax.ppermute(block, PLACE, route)  14.9 us
    ppermute x4, waiting for transfers between devices, move_x(): lax.ppermute(block, 'tp', [(i, (i + 2 * step) % 8) for i in range(8)])  12.4 us
    ppermute x6, starting transfers between devices, swap(): return lax.ppermute(block, PLACE, [(i, i ^ bits) for i in range(32)])  8.72 us
    pallas_call x4, Pallas kernels, project(): pl.pallas_call(functools.partial(project_kernel, spans, shifts, later, he...  6.85 us
    ppermute x4, starting transfers between devices, move_x(): lax.ppermute(block, 'tp', [(i, (i + 2 * step) % 8) for i in range(8)])  4.94 us
    ppermute x1, starting transfers between devices, per_device(): rim = lax.ppermute(row_pairs, PLACE, [(i, i + 1) for i in range(31)])  4.89 us
    unnamed x18, local copies, waits for them, and re-layouts  4.86 us
  transfers between devices with their start and end apart: 23, of which 8 were waited for; matrix products, arithmetic and copies ran while one was open for 4% of the time, Pallas kernels for 35%

profile of v2, /device:TPU:240, one launch (start us, length us, event | category | flops | bytes accessed | tf_op | source)
XLA Modules:
  0.0 97.6 jit_solution(6201195913872672684)
XLA Ops:
  0.6 1.1 %constant_dynamic-update-slice_fusion.1 = bf16[272,1024]{1,0:T(8,128)(2,1)S(1)} fusion(bf16[256,1024]{1,0:T(8,128)(2,1)} %refs_0_.2), kind=kLoop, calls=%fused_computation.9 | loop fusion | bytes 1048576
  1.7 0.8 constant_dynamic-update-slice_fusion
  2.5 0.0 collective-permute-start.2
  2.5 2.8 %collective-permute-start.1 = (bf16[272,1024]{1,0:T(8,128)(2,1)S(1)}, bf16[272,1024]{1,0:T(8,128)(2,1)S(1)}, u32[]{:S(2)}, u32[]{:S(2)}) collective-permute-start(bf16[272,1024]{1,0:T(8,128)(2,1)S(1)} %constant_dynamic-update-slice_fusion), channel_id=1, source_target_pairs={{0,6},{1,7},{2,0},{3,1},{4,2},{5,3},{6,4},{7,5},{8,14},{9,15},{10,... | collective-permute-start | bytes 1671176 | tf_op jit(solution)/shard_map/ppermute | solution.py:49
  5.2 0.0 collective-permute-start
  5.3 0.7 convert_bitcast_fusion
  5.9 0.1 copy.27
  6.0 0.1 broadcast_in_dim.3
  6.2 0.0 copy-start.4
  6.2 0.0 copy-start.5
  6.2 2.8 %copy.32 = bf16[1024,8,2,128]{3,1,2,0:T(8,128)(2,1)S(1)} copy(bf16[1024,8,2,128]{3,2,1,0:T(2,128)(2,1)} %bitcast.18) | data formatting | bytes 8388608
  9.0 0.0 copy-start
  9.0 0.0 copy-start.1
  9.1 0.9 copy-done
  10.0 2.0 %shard_map.104 = (f32[272,256]{1,0:T(8,128)S(1)}, f32[272,128]{1,0:T(8,128)S(1)}) custom-call(s32[1]{0:T(128)} %bitcast.1.tp_ref, bf16[256,1024]{1,0:T(8,128)(2,1)S(1)} %copy-done, bf16[16,1024]{1,0:T(8,128)(2,1)S(1)} %copy-done.1, bf16[272,1024]{1,0:T(8,128)(2,1)S(1)} %collective-permute-done.2.refs_2_, bf16[8192,256]{1,0:T(8,128)(2,1)S(1)} %bitcast.15, ...), custom_call_target="tpu_custom_call" | custom-call | flops 285212672 | bytes 2200000 | tf_op jit(solution)/shard_map/pallas_call | solution.py:152
  12.0 5.8 %collective-permute-done.1.refs_1_ = bf16[272,1024]{1,0:T(8,128)(2,1)S(1)} collective-permute-done((bf16[272,1024]{1,0:T(8,128)(2,1)S(1)}, bf16[272,1024]{1,0:T(8,128)(2,1)S(1)}, u32[]{:S(2)}, u32[]{:S(2)}) %collective-permute-start.1) | collective-permute-done | bytes 557088 | tf_op jit(solution)/shard_map/ppermute | solution.py:49
  17.8 3.4 %collective-permute-done.refs_0_ = bf16[272,1024]{1,0:T(8,128)(2,1)S(1)} collective-permute-done((bf16[272,1024]{1,0:T(8,128)(2,1)S(1)}, bf16[272,1024]{1,0:T(8,128)(2,1)S(1)}, u32[]{:S(2)}, u32[]{:S(2)}) %collective-permute-start) | collective-permute-done | bytes 557088 | tf_op jit(solution)/shard_map/ppermute | solution.py:49
  21.2 0.5 collective-permute-start.6
  21.8 0.4 collective-permute-start.4
  22.1 1.8 %collective-permute-start.3 = (bf16[128,1024]{1,0:T(8,128)(2,1)S(1)}, bf16[128,1024]{1,0:T(8,128)(2,1)S(1)}, u32[]{:S(2)}, u32[]{:S(2)}) collective-permute-start(bf16[128,1024]{1,0:T(8,128)(2,1)S(1)} %slice.12), channel_id=1, source_target_pairs={{0,2},{1,3},{2,4},{3,5},{4,6},{5,7},{6,0},{7,1},{8,10},{9,11},{10,... | collective-permute-start | bytes 786440 | tf_op jit(solution)/shard_map/ppermute | solution.py:49
  24.0 0.0 collective-permute-done.6.refs_3_
  24.0 4.2 %shard_map.105 = (f32[272,256]{1,0:T(8,128)S(1)}, f32[272,128]{1,0:T(8,128)S(1)}, bf16[2,1024,256]{2,1,0:T(8,128)(2,1)S(1)}) custom-call(s32[1]{0:T(128)} %bitcast.1.tp_ref, bf16[272,1024]{1,0:T(8,128)(2,1)S(1)} %collective-permute-done.refs_0_, bf16[272,1024]{1,0:T(8,128)(2,1)S(1)} %collective-permute-done.1.refs_1_, ...), custom_call_target="tpu_custom_call" | custom-call | flops 570425344 | bytes 4400000 | tf_op jit(solution)/shard_map/pallas_call | solution.py:152
  28.1 3.2 %collective-permute-done.3.refs_0_ = bf16[128,1024]{1,0:T(8,128)(2,1)S(1)} collective-permute-done((bf16[128,1024]{1,0:T(8,128)(2,1)S(1)}, bf16[128,1024]{1,0:T(8,128)(2,1)S(1)}, u32[]{:S(2)}, u32[]{:S(2)}) %collective-permute-start.3) | collective-permute-done | bytes 262176 | tf_op jit(solution)/shard_map/ppermute | solution.py:49
  31.4 0.0 collective-permute-done.4.refs_1_
  31.4 0.0 copy-start.2
  31.4 0.1 collective-permute-start.7
  31.5 1.4 %collective-permute-start.12 = (bf16[288,1024]{1,0:T(8,128)(2,1)S(1)}, bf16[288,1024]{1,0:T(8,128)(2,1)S(1)}, u32[]{:S(2)}, u32[]{:S(2)}) collective-permute-start(bf16[288,1024]{1,0:T(8,128)(2,1)S(1)} %fusion.1.refs_1_.refs_5_.refs_2_.refs_3_.refs_12_), channel_id=1, source_target_pairs={{0,32},{8,40},{16,48},{24,56},{32,0},{40,8},{48,16},{56,24},{64,96... | collective-permute-start | bytes 1769480 | tf_op jit(solution)/shard_map/ppermute | solution.py:534
  32.9 0.3 shard_map.106
  33.3 0.2 collective-permute-done.7.refs_0_
  33.5 0.3 shard_map.107
  33.8 1.1 %collective-permute-start.9 = (bf16[256,256]{1,0:T(8,128)(2,1)S(1)}, bf16[256,256]{1,0:T(8,128)(2,1)S(1)}, u32[]{:S(2)}, u32[]{:S(2)}) collective-permute-start(bf16[256,256]{1,0:T(8,128)(2,1)S(1)} %get-tuple-element.87.refs_0_), channel_id=1, source_target_pairs={{0,152},{8,0},{16,8},{24,16},{128,24},{136,128},{144,136},{152,144... | collective-permute-start | bytes 393224 | tf_op jit(solution)/shard_map/ppermute | solution.py:45
  34.9 2.2 %collective-permute-start.8 = (bf16[256,256]{1,0:T(8,128)(2,1)S(1)}, bf16[256,256]{1,0:T(8,128)(2,1)S(1)}, u32[]{:S(2)}, u32[]{:S(2)}) collective-permute-start(bf16[256,256]{1,0:T(8,128)(2,1)S(1)} %get-tuple-element.87.refs_0_), channel_id=1, source_target_pairs={{0,8},{8,16},{16,24},{24,128},{128,136},{136,144},{144,152},{152,0... | collective-permute-start | bytes 393224 | tf_op jit(solution)/shard_map/ppermute | solution.py:45
  37.1 1.6 %shard_map.108 = (f32[2048,128]{1,0:T(8,128)S(1)}, f32[2048,256]{1,0:T(8,128)S(1)}) custom-call(s32[1]{0:T(128)} %bitcast.place_ref, bf16[256,256]{1,0:T(8,128)(2,1)S(1)} %get-tuple-element.87.refs_0_, bf16[288,1024]{1,0:T(8,128)(2,1)S(1)} %fusion.1.refs_1_.refs_5_.refs_2_.refs_3_.refs_12_), custom_call_target="tpu_custom_call" | custom-call | flops 536870912 | bytes 2000000 | tf_op jit(solution)/shard_map/pallas_call | solution.py:450
  38.7 1.9 %collective-permute-done.9.refs_2_ = bf16[256,256]{1,0:T(8,128)(2,1)S(1)} collective-permute-done((bf16[256,256]{1,0:T(8,128)(2,1)S(1)}, bf16[256,256]{1,0:T(8,128)(2,1)S(1)}, u32[]{:S(2)}, u32[]{:S(2)}) %collective-permute-start.9) | collective-permute-done | bytes 131104 | tf_op jit(solution)/shard_map/ppermute | solution.py:45
  40.7 0.0 collective-permute-done.8.refs_1_
  40.7 3.0 %collective-permute-start.10 = (bf16[256,256]{1,0:T(8,128)(2,1)S(1)}, bf16[256,256]{1,0:T(8,128)(2,1)S(1)}, u32[]{:S(2)}, u32[]{:S(2)}) collective-permute-start(bf16[256,256]{1,0:T(8,128)(2,1)S(1)} %collective-permute-done.8.refs_1_), channel_id=1, source_target_pairs={{0,8},{8,16},{16,24},{24,128},{128,136},{136,144},{144,152},{152,0... | collective-permute-start | bytes 393224 | tf_op jit(solution)/shard_map/ppermute | solution.py:45
  43.6 0.0 collective-permute-start.11
  43.6 4.9 %collective-permute-start.13 = (bf16[16,256]{1,0:T(8,128)(2,1)S(1)}, bf16[16,256]{1,0:T(8,128)(2,1)S(1)}, u32[]{:S(2)}, u32[]{:S(2)}) collective-permute-start(bf16[16,256]{1,0:T(8,128)(2,1)S(1)} %get-tuple-element.94.refs_15_), channel_id=1, source_target_pairs={{0,8},{8,16},{16,24},{24,32},{32,40},{40,48},{48,56},{56,64},{64,7... | collective-permute-start | bytes 24584 | tf_op jit(solution)/shard_map/ppermute | solution.py:574
  48.5 0.8 collective-permute-start.14
  49.4 0.5 collective-permute-done.13.refs_14_
  49.9 0.0 collective-permute-done.10.refs_3_
  49.9 0.0 collective-permute-done.11.refs_4_
  49.9 5.3 %collective-permute-start.16 = (bf16[256,256]{1,0:T(8,128)(2,1)S(1)}, bf16[256,256]{1,0:T(8,128)(2,1)S(1)}, u32[]{:S(2)}, u32[]{:S(2)}) collective-permute-start(bf16[256,256]{1,0:T(8,128)(2,1)S(1)} %collective-permute-done.10.refs_3_), channel_id=1, source_target_pairs={{0,8},{8,16},{16,24},{24,128},{128,136},{136,144},{144,152},{152,0... | collective-permute-start | bytes 393224 | tf_op jit(solution)/shard_map/ppermute | solution.py:45
  55.2 0.0 collective-permute-start.17
  55.2 0.4 collective-permute-start.15
  55.7 4.9 %shard_map.109 = (f32[2048,128]{1,0:T(8,128)S(1)}, f32[2048,256]{1,0:T(8,128)S(1)}, f32[256,128]{1,0:T(8,128)S(1)}, f32[256,256]{1,0:T(8,128)S(1)}) custom-call(s32[1]{0:T(128)} %bitcast.place_ref, bf16[256,256]{1,0:T(8,128)(2,1)S(1)} %get-tuple-element.87.refs_0_, bf16[256,256]{1,0:T(8,128)(2,1)S(1)} %collective-permute-done.8.refs_1_, ...), custom_call_target="tpu_custom_call" | custom-call | flops 2684354560 | bytes 2000000 | tf_op jit(solution)/shard_map/pallas_call | solution.py:450
  60.5 1.0 %collective-permute-done.17.refs_1_.refs_8_ = bf16[256,256]{1,0:T(8,128)(2,1)S(1)} collective-permute-done((bf16[256,256]{1,0:T(8,128)(2,1)S(1)}, bf16[256,256]{1,0:T(8,128)(2,1)S(1)}, u32[]{:S(2)}, u32[]{:S(2)}) %collective-permute-start.17) | collective-permute-done | bytes 131104 | tf_op jit(solution)/shard_map/ppermute | solution.py:45
  61.6 0.1 collective-permute-start.19
  61.7 3.2 %collective-permute-start.18 = (bf16[128,256]{1,0:T(8,128)(2,1)S(1)}, bf16[128,256]{1,0:T(8,128)(2,1)S(1)}, u32[]{:S(2)}, u32[]{:S(2)}) collective-permute-start(bf16[128,256]{1,0:T(8,128)(2,1)S(1)} %slice.14), channel_id=1, source_target_pairs={{0,8},{8,16},{16,24},{24,128},{128,136},{136,144},{144,152},{152,0... | collective-permute-start | bytes 196616 | tf_op jit(solution)/shard_map/ppermute | solution.py:45
  64.9 0.8 collective-permute-start.20
  65.8 0.0 collective-permute-done.15.refs_1_.refs_6_
  65.8 0.0 collective-permute-done.14.refs_0_.refs_5_
  65.8 4.5 %shard_map.110 = (f32[2048,128]{1,0:T(8,128)S(1)}, f32[2048,256]{1,0:T(8,128)S(1)}, f32[256,128]{1,0:T(8,128)S(1)}, f32[256,256]{1,0:T(8,128)S(1)}) custom-call(s32[1]{0:T(128)} %bitcast.place_ref, bf16[768,256]{1,0:T(8,128)(2,1)S(1)} %collective-permute-done.14.refs_0_.refs_5_, ...), custom_call_target="tpu_custom_call", output_to_operand_aliasing={{0}: (5, {}), {1}: (6, {}), {2}: (7, {}), {3}: (8, {})} | custom-call | flops 2684354560 | bytes 2000000 | tf_op jit(solution)/shard_map/pallas_call | solution.py:450
  70.3 0.0 collective-permute-done.19
  70.3 0.0 collective-permute-done.18
  70.3 1.6 %collective-permute-start.21 = (bf16[256,256]{1,0:T(8,128)(2,1)S(1)}, bf16[256,256]{1,0:T(8,128)(2,1)S(1)}, u32[]{:S(2)}, u32[]{:S(2)}) collective-permute-start(bf16[256,256]{1,0:T(8,128)(2,1)S(1)} %constant_dynamic-update-slice_fusion.2.refs_2_.refs_9_), channel_id=1, source_target_pairs={{0,96},{8,104},{16,112},{24,120},{32,64},{40,72},{48,80},{56,88},{... | collective-permute-start | bytes 393224 | tf_op jit(solution)/shard_map/ppermute | solution.py:534
  71.9 3.1 %shard_map.111 = (f32[2048,128]{1,0:T(8,128)S(1)}, f32[2048,256]{1,0:T(8,128)S(1)}, f32[256,128]{1,0:T(8,128)S(1)}, f32[256,256]{1,0:T(8,128)S(1)}) custom-call(s32[1]{0:T(128)} %bitcast.place_ref, bf16[256,256]{1,0:T(8,128)(2,1)S(1)} %collective-permute-done.16.refs_0_.refs_7_, ...), custom_call_target="tpu_custom_call", output_to_operand_aliasing={{0}: (6, {}), {1}: (7, {}), {2}: (8, {}), {3}: (9, {})} | custom-call | flops 1610612736 | bytes 2000000 | tf_op jit(solution)/shard_map/pallas_call | solution.py:450
  75.0 0.6 collective-permute-done.21.refs_1_.refs_11_
  75.6 0.0 collective-permute-done.20.refs_0_.refs_10_
  75.6 3.5 %shard_map.112 = (bf16[2272,128]{1,0:T(8,128)(2,1)S(1)}, f32[2048,128]{1,0:T(8,128)S(1)}, f32[2048,256]{1,0:T(8,128)S(1)}, f32[256,128]{1,0:T(8,128)S(1)}, f32[256,256]{1,0:T(8,128)S(1)}) custom-call(s32[1]{0:T(128)} %bitcast.place_ref, ...), custom_call_target="tpu_custom_call", output_to_operand_aliasing={{1}: (5, {}), {2}: (6, {}), {3}: (7, {}), {4}: (8, {})} | custom-call | flops 1610612736 | bytes 2000000 | tf_op jit(solution)/shard_map/pallas_call | solution.py:450
  79.1 3.7 %collective-permute-start.22 = (bf16[2272,128]{1,0:T(8,128)(2,1)S(1)}, bf16[2272,128]{1,0:T(8,128)(2,1)S(1)}, u32[]{:S(2)}, u32[]{:S(2)}) collective-permute-start(bf16[2272,128]{1,0:T(8,128)(2,1)S(1)} %get-tuple-element.127), channel_id=1, source_target_pairs={{0,32},{8,40},{16,48},{24,56},{32,0},{40,8},{48,16},{56,24},{64,96... | collective-permute-start | bytes 1744904 | tf_op jit(solution)/shard_map/ppermute | solution.py:534
  82.8 13.3 %shard_map.113 = (f32[2048,128]{1,0:T(8,128)S(1)}, f32[2048,256]{1,0:T(8,128)S(1)}, f32[256,128]{1,0:T(8,128)S(1)}, f32[256,256]{1,0:T(8,128)S(1)}) custom-call(s32[1]{0:T(128)} %bitcast.place_ref, s32[512]{0:T(512)S(1)} %copy-done.3, ...), custom_call_target="tpu_custom_call", output_to_operand_aliasing={{0}: (17, {}), {1}: (18, {}), {2}: (19, {}), {3}: (20, {})} | custom-call | flops 8053063680 | bytes 2000000 | tf_op jit(solution)/shard_map/pallas_call | solution.py:450
  96.2 0.0 collective-permute-done.22.packed
  96.2 1.4 %shard_map.114 = (bf16[256,1024]{1,0:T(8,128)(2,1)}, bf16[16,1024]{1,0:T(8,128)(2,1)}) custom-call(f32[2048,128]{1,0:T(8,128)S(1)} %get-tuple-element.136.own_top, f32[2048,256]{1,0:T(8,128)S(1)} %get-tuple-element.137.own_mixed, f32[256,128]{1,0:T(8,128)S(1)} %get-tuple-element.138.rows_top, f32[256,256]{1,0:T(8,128)S(1)} %get-tuple-element.139.rows_mixed, ...), custom_call_target="tpu_custom_call" | custom-call | tf_op jit(solution)/shard_map/pallas_call | solution.py:504
  (27 shorter events, 0.3 us)
Async XLA Ops:
  0.6 5.5 %copy-start.6 = (f32[8192]{0:T(1024)S(1)}, f32[8192]{0:T(1024)}, u32[]{:S(2)}) copy-start(f32[8192]{0:T(1024)} %param.11) | copy-start | bytes 98308
  2.5 6.6 %collective-permute-start.2 = (bf16[272,1024]{1,0:T(8,128)(2,1)S(1)}, bf16[272,1024]{1,0:T(8,128)(2,1)S(1)}, u32[]{:S(2)}, u32[]{:S(2)}) collective-permute-start(bf16[272,1024]{1,0:T(8,128)(2,1)S(1)} %constant_dynamic-update-slice_fusion), channel_id=1, source_target_pairs={{0,1},{1,0},{2,3},{3,2},{4,5},{5,4},{6,7},{7,6},{8,9},{9,8},{10,11... | collective-permute-start | bytes 1671176 | tf_op jit(solution)/shard_map/ppermute | solution.py:53
  2.5 15.3 %collective-permute-start.1 = (bf16[272,1024]{1,0:T(8,128)(2,1)S(1)}, bf16[272,1024]{1,0:T(8,128)(2,1)S(1)}, u32[]{:S(2)}, u32[]{:S(2)}) collective-permute-start(bf16[272,1024]{1,0:T(8,128)(2,1)S(1)} %constant_dynamic-update-slice_fusion), channel_id=1, source_target_pairs={{0,6},{1,7},{2,0},{3,1},{4,2},{5,3},{6,4},{7,5},{8,14},{9,15},{10,... | collective-permute-start | bytes 1671176 | tf_op jit(solution)/shard_map/ppermute | solution.py:49
  5.2 16.0 %collective-permute-start = (bf16[272,1024]{1,0:T(8,128)(2,1)S(1)}, bf16[272,1024]{1,0:T(8,128)(2,1)S(1)}, u32[]{:S(2)}, u32[]{:S(2)}) collective-permute-start(bf16[272,1024]{1,0:T(8,128)(2,1)S(1)} %constant_dynamic-update-slice_fusion), channel_id=1, source_target_pairs={{0,2},{1,3},{2,4},{3,5},{4,6},{5,7},{6,0},{7,1},{8,10},{9,11},{10,... | collective-permute-start | bytes 1671176 | tf_op jit(solution)/shard_map/ppermute | solution.py:49
  6.2 2.8 %copy-start.4 = (bf16[256,1024]{1,0:T(8,128)(2,1)S(1)}, bf16[256,1024]{1,0:T(8,128)(2,1)}, u32[]{:S(2)}) copy-start(bf16[256,1024]{1,0:T(8,128)(2,1)} %param.14) | copy-start | bytes 1572868
  6.2 2.8 %copy-start.5 = (bf16[16,1024]{1,0:T(8,128)(2,1)S(1)}, bf16[16,1024]{1,0:T(8,128)(2,1)}, u32[]{:S(2)}) copy-start(bf16[16,1024]{1,0:T(8,128)(2,1)} %param.15) | copy-start | bytes 98308
  9.0 1.0 %copy-start = (bf16[256,1024]{1,0:T(8,128)(2,1)S(1)}, bf16[256,1024]{1,0:T(8,128)(2,1)}, u32[]{:S(2)}) copy-start(bf16[256,1024]{1,0:T(8,128)(2,1)} %refs_0_.2) | copy-start | bytes 1572868
  9.0 1.0 %copy-start.1 = (bf16[16,1024]{1,0:T(8,128)(2,1)S(1)}, bf16[16,1024]{1,0:T(8,128)(2,1)}, u32[]{:S(2)}) copy-start(bf16[16,1024]{1,0:T(8,128)(2,1)} %refs_1_.1) | copy-start | bytes 98308
  21.2 2.7 %collective-permute-start.5 = (bf16[272,1024]{1,0:T(8,128)(2,1)S(1)}, bf16[272,1024]{1,0:T(8,128)(2,1)S(1)}, u32[]{:S(2)}, u32[]{:S(2)}) collective-permute-start(bf16[272,1024]{1,0:T(8,128)(2,1)S(1)} %collective-permute-done.refs_0_), channel_id=1, source_target_pairs={{0,1},{1,0},{2,3},{3,2},{4,5},{5,4},{6,7},{7,6},{8,9},{9,8},{10,11... | collective-permute-start | bytes 1671176 | tf_op jit(solution)/shard_map/ppermute | solution.py:53
  21.2 2.8 %collective-permute-start.6 = (bf16[272,1024]{1,0:T(8,128)(2,1)S(1)}, bf16[272,1024]{1,0:T(8,128)(2,1)S(1)}, u32[]{:S(2)}, u32[]{:S(2)}) collective-permute-start(bf16[272,1024]{1,0:T(8,128)(2,1)S(1)} %collective-permute-done.1.refs_1_), channel_id=1, source_target_pairs={{0,1},{1,0},{2,3},{3,2},{4,5},{5,4},{6,7},{7,6},{8,9},{9,8},{10,11... | collective-permute-start | bytes 1671176 | tf_op jit(solution)/shard_map/ppermute | solution.py:53
  21.8 9.6 %collective-permute-start.4 = (bf16[144,1024]{1,0:T(8,128)(2,1)S(1)}, bf16[144,1024]{1,0:T(8,128)(2,1)S(1)}, u32[]{:S(2)}, u32[]{:S(2)}) collective-permute-start(bf16[144,1024]{1,0:T(8,128)(2,1)S(1)} %slice.13), channel_id=1, source_target_pairs={{0,6},{1,7},{2,0},{3,1},{4,2},{5,3},{6,4},{7,5},{8,14},{9,15},{10,... | collective-permute-start | bytes 884744 | tf_op jit(solution)/shard_map/ppermute | solution.py:49
  22.1 9.2 %collective-permute-start.3 = (bf16[128,1024]{1,0:T(8,128)(2,1)S(1)}, bf16[128,1024]{1,0:T(8,128)(2,1)S(1)}, u32[]{:S(2)}, u32[]{:S(2)}) collective-permute-start(bf16[128,1024]{1,0:T(8,128)(2,1)S(1)} %slice.12), channel_id=1, source_target_pairs={{0,2},{1,3},{2,4},{3,5},{4,6},{5,7},{6,0},{7,1},{8,10},{9,11},{10,... | collective-permute-start | bytes 786440 | tf_op jit(solution)/shard_map/ppermute | solution.py:49
  31.4 2.1 %copy-start.2 = (f32[128]{0:T(128)S(1)}, f32[128]{0:T(128)}, u32[]{:S(2)}) copy-start(f32[128]{0:T(128)} %param.13) | copy-start | bytes 1540
  31.4 2.0 %collective-permute-start.7 = (bf16[272,1024]{1,0:T(8,128)(2,1)S(1)}, bf16[272,1024]{1,0:T(8,128)(2,1)S(1)}, u32[]{:S(2)}, u32[]{:S(2)}) collective-permute-start(bf16[272,1024]{1,0:T(8,128)(2,1)S(1)} %pad_maximum_fusion), channel_id=1, source_target_pairs={{0,1},{1,0},{2,3},{3,2},{4,5},{5,4},{6,7},{7,6},{8,9},{9,8},{10,11... | collective-permute-start | bytes 1671176 | tf_op jit(solution)/shard_map/ppermute | solution.py:53
  31.5 17.9 %collective-permute-start.12 = (bf16[288,1024]{1,0:T(8,128)(2,1)S(1)}, bf16[288,1024]{1,0:T(8,128)(2,1)S(1)}, u32[]{:S(2)}, u32[]{:S(2)}) collective-permute-start(bf16[288,1024]{1,0:T(8,128)(2,1)S(1)} %fusion.1.refs_1_.refs_5_.refs_2_.refs_3_.refs_12_), channel_id=1, source_target_pairs={{0,32},{8,40},{16,48},{24,56},{32,0},{40,8},{48,16},{56,24},{64,96... | collective-permute-start | bytes 1769480 | tf_op jit(solution)/shard_map/ppermute | solution.py:534
  33.8 6.8 %collective-permute-start.9 = (bf16[256,256]{1,0:T(8,128)(2,1)S(1)}, bf16[256,256]{1,0:T(8,128)(2,1)S(1)}, u32[]{:S(2)}, u32[]{:S(2)}) collective-permute-start(bf16[256,256]{1,0:T(8,128)(2,1)S(1)} %get-tuple-element.87.refs_0_), channel_id=1, source_target_pairs={{0,152},{8,0},{16,8},{24,16},{128,24},{136,128},{144,136},{152,144... | collective-permute-start | bytes 393224 | tf_op jit(solution)/shard_map/ppermute | solution.py:45
  34.9 5.7 %collective-permute-start.8 = (bf16[256,256]{1,0:T(8,128)(2,1)S(1)}, bf16[256,256]{1,0:T(8,128)(2,1)S(1)}, u32[]{:S(2)}, u32[]{:S(2)}) collective-permute-start(bf16[256,256]{1,0:T(8,128)(2,1)S(1)} %get-tuple-element.87.refs_0_), channel_id=1, source_target_pairs={{0,8},{8,16},{16,24},{24,128},{128,136},{136,144},{144,152},{152,0... | collective-permute-start | bytes 393224 | tf_op jit(solution)/shard_map/ppermute | solution.py:45
  40.7 9.2 %collective-permute-start.10 = (bf16[256,256]{1,0:T(8,128)(2,1)S(1)}, bf16[256,256]{1,0:T(8,128)(2,1)S(1)}, u32[]{:S(2)}, u32[]{:S(2)}) collective-permute-start(bf16[256,256]{1,0:T(8,128)(2,1)S(1)} %collective-permute-done.8.refs_1_), channel_id=1, source_target_pairs={{0,8},{8,16},{16,24},{24,128},{128,136},{136,144},{144,152},{152,0... | collective-permute-start | bytes 393224 | tf_op jit(solution)/shard_map/ppermute | solution.py:45
  43.6 6.2 %collective-permute-start.11 = (bf16[256,256]{1,0:T(8,128)(2,1)S(1)}, bf16[256,256]{1,0:T(8,128)(2,1)S(1)}, u32[]{:S(2)}, u32[]{:S(2)}) collective-permute-start(bf16[256,256]{1,0:T(8,128)(2,1)S(1)} %collective-permute-done.9.refs_2_), channel_id=1, source_target_pairs={{0,152},{8,0},{16,8},{24,16},{128,24},{136,128},{144,136},{152,144... | collective-permute-start | bytes 393224 | tf_op jit(solution)/shard_map/ppermute | solution.py:45
  43.6 6.2 %collective-permute-start.13 = (bf16[16,256]{1,0:T(8,128)(2,1)S(1)}, bf16[16,256]{1,0:T(8,128)(2,1)S(1)}, u32[]{:S(2)}, u32[]{:S(2)}) collective-permute-start(bf16[16,256]{1,0:T(8,128)(2,1)S(1)} %get-tuple-element.94.refs_15_), channel_id=1, source_target_pairs={{0,8},{8,16},{16,24},{24,32},{32,40},{40,48},{48,56},{56,64},{64,7... | collective-permute-start | bytes 24584 | tf_op jit(solution)/shard_map/ppermute | solution.py:574
  48.5 17.2 %collective-permute-start.14 = (bf16[768,256]{1,0:T(8,128)(2,1)S(1)}, bf16[768,256]{1,0:T(8,128)(2,1)S(1)}, u32[]{:S(2)}, u32[]{:S(2)}) collective-permute-start(bf16[768,256]{1,0:T(8,128)(2,1)S(1)} %pad_maximum_fusion.1), channel_id=1, source_target_pairs={{0,96},{8,104},{16,112},{24,120},{32,64},{40,72},{48,80},{56,88},{... | collective-permute-start | bytes 1179656 | tf_op jit(solution)/shard_map/ppermute | solution.py:534
  49.9 10.7 %collective-permute-start.16 = (bf16[256,256]{1,0:T(8,128)(2,1)S(1)}, bf16[256,256]{1,0:T(8,128)(2,1)S(1)}, u32[]{:S(2)}, u32[]{:S(2)}) collective-permute-start(bf16[256,256]{1,0:T(8,128)(2,1)S(1)} %collective-permute-done.10.refs_3_), channel_id=1, source_target_pairs={{0,8},{8,16},{16,24},{24,128},{128,136},{136,144},{144,152},{152,0... | collective-permute-start | bytes 393224 | tf_op jit(solution)/shard_map/ppermute | solution.py:45
  55.2 6.4 %collective-permute-start.17 = (bf16[256,256]{1,0:T(8,128)(2,1)S(1)}, bf16[256,256]{1,0:T(8,128)(2,1)S(1)}, u32[]{:S(2)}, u32[]{:S(2)}) collective-permute-start(bf16[256,256]{1,0:T(8,128)(2,1)S(1)} %collective-permute-done.11.refs_4_), channel_id=1, source_target_pairs={{0,152},{8,0},{16,8},{24,16},{128,24},{136,128},{144,136},{152,144... | collective-permute-start | bytes 393224 | tf_op jit(solution)/shard_map/ppermute | solution.py:45
  55.2 10.5 %collective-permute-start.15 = (bf16[512,256]{1,0:T(8,128)(2,1)S(1)}, bf16[512,256]{1,0:T(8,128)(2,1)S(1)}, u32[]{:S(2)}, u32[]{:S(2)}) collective-permute-start(bf16[512,256]{1,0:T(8,128)(2,1)S(1)} %pad_maximum_fusion.2), channel_id=1, source_target_pairs={{0,96},{8,104},{16,112},{24,120},{32,64},{40,72},{48,80},{56,88},{... | collective-permute-start | bytes 786440 | tf_op jit(solution)/shard_map/ppermute | solution.py:534
  61.6 8.7 %collective-permute-start.19 = (bf16[128,256]{1,0:T(8,128)(2,1)S(1)}, bf16[128,256]{1,0:T(8,128)(2,1)S(1)}, u32[]{:S(2)}, u32[]{:S(2)}) collective-permute-start(bf16[128,256]{1,0:T(8,128)(2,1)S(1)} %slice.15), channel_id=1, source_target_pairs={{0,152},{8,0},{16,8},{24,16},{128,24},{136,128},{144,136},{152,144... | collective-permute-start | bytes 196616 | tf_op jit(solution)/shard_map/ppermute | solution.py:45
  61.7 8.6 %collective-permute-start.18 = (bf16[128,256]{1,0:T(8,128)(2,1)S(1)}, bf16[128,256]{1,0:T(8,128)(2,1)S(1)}, u32[]{:S(2)}, u32[]{:S(2)}) collective-permute-start(bf16[128,256]{1,0:T(8,128)(2,1)S(1)} %slice.14), channel_id=1, source_target_pairs={{0,8},{8,16},{16,24},{24,128},{128,136},{136,144},{144,152},{152,0... | collective-permute-start | bytes 196616 | tf_op jit(solution)/shard_map/ppermute | solution.py:45
  64.9 10.7 %collective-permute-start.20 = (bf16[512,256]{1,0:T(8,128)(2,1)S(1)}, bf16[512,256]{1,0:T(8,128)(2,1)S(1)}, u32[]{:S(2)}, u32[]{:S(2)}) collective-permute-start(bf16[512,256]{1,0:T(8,128)(2,1)S(1)} %pad_maximum_fusion.3), channel_id=1, source_target_pairs={{0,96},{8,104},{16,112},{24,120},{32,64},{40,72},{48,80},{56,88},{... | collective-permute-start | bytes 786440 | tf_op jit(solution)/shard_map/ppermute | solution.py:534
  70.3 5.3 %collective-permute-start.21 = (bf16[256,256]{1,0:T(8,128)(2,1)S(1)}, bf16[256,256]{1,0:T(8,128)(2,1)S(1)}, u32[]{:S(2)}, u32[]{:S(2)}) collective-permute-start(bf16[256,256]{1,0:T(8,128)(2,1)S(1)} %constant_dynamic-update-slice_fusion.2.refs_2_.refs_9_), channel_id=1, source_target_pairs={{0,96},{8,104},{16,112},{24,120},{32,64},{40,72},{48,80},{56,88},{... | collective-permute-start | bytes 393224 | tf_op jit(solution)/shard_map/ppermute | solution.py:534
  75.6 7.2 %copy-start.3 = (s32[512]{0:T(512)S(1)}, s32[512]{0:T(512)}, u32[]{:S(2)}) copy-start(s32[512]{0:T(512)} %refs_0_.3) | copy-start | bytes 6148
  79.1 17.0 %collective-permute-start.22 = (bf16[2272,128]{1,0:T(8,128)(2,1)S(1)}, bf16[2272,128]{1,0:T(8,128)(2,1)S(1)}, u32[]{:S(2)}, u32[]{:S(2)}) collective-permute-start(bf16[2272,128]{1,0:T(8,128)(2,1)S(1)} %get-tuple-element.127), channel_id=1, source_target_pairs={{0,32},{8,40},{16,48},{24,56},{32,0},{40,8},{48,16},{56,24},{64,96... | collective-permute-start | bytes 1744904 | tf_op jit(solution)/shard_map/ppermute | solution.py:534
